TPU v7x, 1024 devices: a whole 4x4x32 slice. The times are simulated.
1024 devices in a mesh: tile: 64 (over z, core), band: 16 (over x, y).
Axes of the slice: x: 4, y: 4, z: 32, core: 2. Of those that a mesh axis runs over, the one named last changes fastest.
Arguments:
- ocean_velocity: float32 [2, 8, 256, 8192], P(None, None, 'band', 'tile'), may hold values from -6 to 6
- ocean_wet: int32 [256, 8192], P('band', 'tile'), may hold values 0 or 1
- coriolis: float32 [256], P('band'), may hold values from -2 to 2
- spectrum: float32 [128, 1024, 1296], P('band', 'tile'), may hold values from 0.05 to 2
- group_speed: float32 [36], replicated, may hold values from 0.5 to 2
- source_matrix: bfloat16 [1296, 1296], replicated, may hold values from -0.15625 to 0.15625
- moments: float32 [4, 1296], replicated, may hold values from -0.15625 to 0.15625
- o2w_rows: int32 [64, 16, 64, 2], P('tile', 'band'), may hold values from 0 to 31
- ocean_to_wave_index: int32 [4, 128, 1024], P(None, 'band', 'tile'), may hold values from 0 to 16383
- o2w_weight: int32 [4, 128, 1024], P(None, 'band', 'tile'), may hold values from 1 to 8
- w2o_rows: int32 [64, 16, 64, 1], P('tile', 'band'), may hold values from 0 to 1
- wave_to_ocean_index: int32 [4, 256, 8192], P(None, 'band', 'tile'), may hold values from 0 to 8191
- wave_to_ocean_weight: int32 [4, 256, 8192], P(None, 'band', 'tile'), may hold values from 1 to 8
Outputs:
- ocean_next: float32 [2, 8, 256, 8192], P(None, None, 'band', 'tile')
- spectrum_next: float32 [128, 1024, 1296], P('band', 'tile')
Inputs may be any that keep to these rules, and one draw needn't show every extreme that they name: `o2w_rows`: entries below 16 name a row of the sending ocean block; larger entries mark an empty slot. `ocean_to_wave_index`: index into the wave block's received buffer of 64 x 2 x 128 entries. `w2o_rows`: entries below 1 name a list row of the sending wave block; larger entries mark an empty slot. `wave_to_ocean_index`: index into the ocean block's received buffer of 64 x 1 x 128 entries.
All inputs are finite; a program needn't handle non-finite values. No bound on the sum of `ocean_wet` on one device may be relied on, other than what follows from the above.
Results may differ from a plain program's by a relative error of at most 0.001.
Values sent between devices are 32-bit elements; how exact they have to be, the bound alone decides.
A program may use at most 64 MiB of HBM per device.

v0:
```python
import math

import jax
import jax.numpy as jnp
from jax import lax
from jax.sharding import PartitionSpec as P

NDIR = 36
NFREQ = 36
WSTEPS = 2


DT_OCEAN = 0.2
VISCOSITY = 0.5
VERT_FRICTION = 0.5
STRESS_COEFF = 1.0
DT_WAVE = 0.1
DT_SOURCE = 0.3


def with_halo(block, sides, width):
    for axis, dim in sides:
        count = lax.axis_size(axis)
        forward = [(i, i + 1) for i in range(count - 1)]
        backward = [(target, source) for source, target in forward]
        low = lax.ppermute(
            lax.slice_in_dim(block, block.shape[dim] - width, None, axis=dim), axis, forward
        )
        high = lax.ppermute(lax.slice_in_dim(block, 0, width, axis=dim), axis, backward)
        block = jnp.concatenate([low, block, high], axis=dim)
    return block


def bin_speeds(group_speed):
    angle = (jnp.arange(NDIR, dtype=jnp.float32) + 0.5) * (2.0 * math.pi / NDIR)
    speed_x = (jnp.cos(angle)[:, None] * group_speed[None, :]).reshape(NDIR * NFREQ)
    speed_y = (jnp.sin(angle)[:, None] * group_speed[None, :]).reshape(NDIR * NFREQ)
    return (speed_x, speed_y)


def advance(padded, current_x, current_y, speed_x, speed_y, source_matrix):
    center = padded[1:-1, 1:-1]
    west_side = padded[1:-1, :-2]
    east_side = padded[1:-1, 2:]
    south_side = padded[:-2, 1:-1]
    north_side = padded[2:, 1:-1]
    flow_x = speed_x + current_x[:, :, None]
    flow_y = speed_y + current_y[:, :, None]
    change = (
        jnp.maximum(flow_x, 0.0) * (center - west_side)
        + jnp.minimum(flow_x, 0.0) * (east_side - center)
        + jnp.maximum(flow_y, 0.0) * (center - south_side)
        + jnp.minimum(flow_y, 0.0) * (north_side - center)
    )
    moved = center - DT_WAVE * change
    rounded = moved.astype(jnp.bfloat16)
    source = jnp.dot(
        rounded.reshape(-1, moved.shape[2]), source_matrix, preferred_element_type=jnp.float32
    )
    return moved + DT_SOURCE * source.reshape(moved.shape)


def weighted_pick(buffer, index, weight):
    values = buffer[:, index]
    factor = weight.astype(jnp.float32)
    return jnp.sum(values * factor[None], axis=1) / jnp.sum(factor, axis=0)


def ocean_update(velocity, padded, wet, coriolis, forcing_field):
    laplace = (
        padded[:, :, :-2, 1:-1]
        + padded[:, :, 2:, 1:-1]
        + padded[:, :, 1:-1, :-2]
        + padded[:, :, 1:-1, 2:]
        - 4.0 * velocity
    )
    above = jnp.concatenate([velocity[:, :1], velocity[:, :-1]], axis=1)
    below = jnp.concatenate([velocity[:, 1:], velocity[:, -1:]], axis=1)
    vertical = above - 2.0 * velocity + below
    rotation = coriolis[:, None]
    turning = jnp.stack([rotation * velocity[1], -rotation * velocity[0]])
    tendency = VISCOSITY * laplace + VERT_FRICTION * vertical + turning
    surface_layer = jnp.stack(
        [
            STRESS_COEFF * forcing_field[0] + rotation * forcing_field[3],
            STRESS_COEFF * forcing_field[1] - rotation * forcing_field[2],
        ]
    )
    tendency = tendency.at[:, 0].add(surface_layer)
    return wet.astype(jnp.float32) * (velocity + DT_OCEAN * tendency)


def on_device(
    ocean_velocity,
    ocean_wet,
    coriolis,
    spectrum,
    group_speed,
    source_matrix,
    moments,
    o2w_rows,
    ocean_to_wave_index,
    o2w_weight,
    w2o_rows,
    wave_to_ocean_index,
    wave_to_ocean_weight,
):
    ocean_rows = ocean_velocity.shape[2]
    row_length = ocean_velocity.shape[3]
    height, width, bins = spectrum.shape
    ocean_padded = with_halo(ocean_velocity, (("tile", 3), ("band", 2)), 1)
    surface_layer = ocean_velocity[:, 0].transpose(1, 0, 2)
    surface_layer = jnp.concatenate(
        [surface_layer, jnp.zeros((1,) + surface_layer.shape[1:], jnp.float32)], axis=0
    )
    outgoing = jnp.take(surface_layer, jnp.minimum(o2w_rows[0, 0], ocean_rows), axis=0)
    incoming = lax.all_to_all(outgoing, "tile", split_axis=0, concat_axis=0, tiled=True)
    current_buffer = incoming.transpose(2, 0, 1, 3).reshape(2, -1)
    currents = weighted_pick(
        current_buffer,
        ocean_to_wave_index.reshape(ocean_to_wave_index.shape[0], -1),
        o2w_weight.reshape(o2w_weight.shape[0], -1),
    ).reshape(2, height, width)
    speed_x, speed_y = bin_speeds(group_speed)
    spectrum_now = spectrum
    for step in range(WSTEPS):
        padded = with_halo(spectrum_now, (("tile", 1), ("band", 0)), 1)
        spectrum_now = advance(padded, currents[0], currents[1], speed_x, speed_y, source_matrix)
    total_sums = jnp.einsum("yxb,qb->qyx", spectrum_now, moments, precision=lax.Precision.HIGHEST)
    total_sums = total_sums.reshape(4, -1, row_length)
    block_count = total_sums.shape[1]
    total_sums = jnp.concatenate(
        [total_sums, jnp.zeros((4, 1, row_length), jnp.float32)], axis=1
    ).transpose(1, 0, 2)
    returning = jnp.take(total_sums, jnp.minimum(w2o_rows[0, 0], block_count), axis=0)
    arriving = lax.all_to_all(returning, "tile", split_axis=0, concat_axis=0, tiled=True)
    wave_buffer = arriving.transpose(2, 0, 1, 3).reshape(4, -1)
    forcing_field = weighted_pick(
        wave_buffer,
        wave_to_ocean_index.reshape(wave_to_ocean_index.shape[0], -1),
        wave_to_ocean_weight.reshape(wave_to_ocean_weight.shape[0], -1),
    ).reshape(4, ocean_rows, row_length)
    ocean_next = ocean_update(ocean_velocity, ocean_padded, ocean_wet, coriolis, forcing_field)
    return (ocean_next, spectrum_now)


def solution(mesh):
    placed = (
        P(None, None, "band", "tile"),
        P("band", "tile"),
        P("band"),
        P("band", "tile", None),
        P(),
        P(),
        P(),
        P("tile", "band", None, None),
        P(None, "band", "tile"),
        P(None, "band", "tile"),
        P("tile", "band", None, None),
        P(None, "band", "tile"),
        P(None, "band", "tile"),
    )
    return jax.shard_map(
        on_device,
        mesh=mesh,
        in_specs=placed,
        out_specs=(P(None, None, "band", "tile"), P("band", "tile", None)),
        check_vma=False,
    )
```

profile of v0, /device:TPU:24, one launch (start us, length us, event | category | flops | bytes accessed | tf_op | source)
XLA Modules:
  0.0 198.7 jit_solution(6669008503975598331)
XLA Ops:
  1.8 1.7 collective-permute-start.4
  9.0 33.1 %all-to-all-start = ((f32[64,2,2,128]{3,2,1,0:T(2,128)}), f32[64,2,2,128]{3,2,1,0:T(2,128)S(1)}, u32[]{:S(2)}, u32[]{:S(2)}) async-start(f32[64,2,2,128]{3,2,1,0:T(2,128)} %broadcast_select_fusion), calls=%async_computation | async-start | bytes 262144 | tf_op jit(solution)/shard_map/all_to_all | solution.py:117
  43.1 2.0 collective-permute-start
  53.9 3.1 %collective-permute-start.6 = (f32[1,18,1296]{2,1,0:T(8,128)S(1)}, f32[1,18,1296]{2,1,0:T(8,128)S(1)}, u32[]{:S(2)}, u32[]{:S(2)}) collective-permute-start(f32[1,18,1296]{2,1,0:T(8,128)S(1)} %get-tuple-element.24), channel_id=1, source_target_pairs={{0,1},{1,2},{2,3},{3,4},{4,5},{5,6},{6,7},{7,8},{8,9},{9,10},{10,1... | collective-permute-start | bytes 279944 | tf_op jit(solution)/shard_map/ppermute | solution.py:26
  57.0 2.8 %collective-permute-start.7 = (f32[1,18,1296]{2,1,0:T(8,128)S(1)}, f32[1,18,1296]{2,1,0:T(8,128)S(1)}, u32[]{:S(2)}, u32[]{:S(2)}) collective-permute-start(f32[1,18,1296]{2,1,0:T(8,128)S(1)} %get-tuple-element.25), channel_id=1, source_target_pairs={{1,0},{2,1},{3,2},{4,3},{5,4},{6,5},{7,6},{8,7},{9,8},{10,9},{11,1... | collective-permute-start | bytes 279944 | tf_op jit(solution)/shard_map/ppermute | solution.py:29
  59.8 14.3 %all-to-all-done = f32[64,2,2,128]{3,2,1,0:T(2,128)S(1)} async-done(((f32[64,2,2,128]{3,2,1,0:T(2,128)}), f32[64,2,2,128]{3,2,1,0:T(2,128)S(1)}, u32[]{:S(2)}, u32[]{:S(2)}) %all-to-all-start) | async-done | bytes 131104 | tf_op jit(solution)/shard_map/all_to_all | solution.py:117
  74.1 4.9 %copy.55 = f32[2,64,2,128]{0,3,2,1:T(8,128)} copy(f32[2,64,2,128]{3,0,2,1:T(2,128)S(1)} %bitcast.88) | data formatting | bytes 262144 | tf_op jit(solution)/shard_map/transpose | solution.py:118
  79.0 4.4 %gather_fusion.1 = f32[512,2]{1,0:T(8,128)S(1)} fusion(f32[2,16384]{0,1:T(8,128)} %bitcast.86, s32[1024]{0:T(1024)S(1)} %pad_clamp_fusion.1), kind=kCustom, calls=%fused_computation.1 | custom fusion | bytes 10240 | tf_op jit(solution)/shard_map/gather | solution.py:64
  84.0 3.8 %fusion.7 = f32[8,16,1296]{2,1,0:T(8,128)S(1)} fusion(bf16[1296,1296]{1,0:T(8,128)(2,1)} %param.20, f32[8,16,1296]{2,1,0:T(8,128)S(1)} %copy-done.2, f32[1,18,1296]{2,1,0:T(8,128)S(1)} %collective-permute-done.7, f32[8,1,1296]{2,1,0:T(1,128)S(1)} %collective-permute-done.5, f32[8,1,1296]{2,1,0:T(1,128)S(1)} %collective-permute-done.4, ...), kind=kOutput, calls=%fused_computation.10 | convolution fusion | flops 439437312 | bytes 4967296 | tf_op jit(solution)/shard_map/dot_general | solution.py:57
  90.5 2.6 %collective-permute-done.9 = f32[8,1,1296]{2,1,0:T(1,128)S(1)} collective-permute-done((f32[8,1,1296]{2,1,0:T(1,128)S(1)}, f32[8,1,1296]{2,1,0:T(1,128)S(1)}, u32[]{:S(2)}, u32[]{:S(2)}) %collective-permute-start.9) | collective-permute-done | bytes 41504 | tf_op jit(solution)/shard_map/ppermute | solution.py:29
  93.2 3.1 %collective-permute-start.10 = (f32[1,18,1296]{2,1,0:T(8,128)S(1)}, f32[1,18,1296]{2,1,0:T(8,128)S(1)}, u32[]{:S(2)}, u32[]{:S(2)}) collective-permute-start(f32[1,18,1296]{2,1,0:T(8,128)S(1)} %get-tuple-element.22), channel_id=1, source_target_pairs={{0,1},{1,2},{2,3},{3,4},{4,5},{5,6},{6,7},{7,8},{8,9},{9,10},{10,1... | collective-permute-start | bytes 279944 | tf_op jit(solution)/shard_map/ppermute | solution.py:26
  96.2 2.8 %collective-permute-start.11 = (f32[1,18,1296]{2,1,0:T(8,128)S(1)}, f32[1,18,1296]{2,1,0:T(8,128)S(1)}, u32[]{:S(2)}, u32[]{:S(2)}) collective-permute-start(f32[1,18,1296]{2,1,0:T(8,128)S(1)} %get-tuple-element.23), channel_id=1, source_target_pairs={{1,0},{2,1},{3,2},{4,3},{5,4},{6,5},{7,6},{8,7},{9,8},{10,9},{11,1... | collective-permute-start | bytes 279944 | tf_op jit(solution)/shard_map/ppermute | solution.py:29
  100.1 5.2 %collective-permute-done.11 = f32[1,18,1296]{2,1,0:T(8,128)S(1)} collective-permute-done((f32[1,18,1296]{2,1,0:T(8,128)S(1)}, f32[1,18,1296]{2,1,0:T(8,128)S(1)}, u32[]{:S(2)}, u32[]{:S(2)}) %collective-permute-start.11) | collective-permute-done | bytes 93344 | tf_op jit(solution)/shard_map/ppermute | solution.py:29
  105.2 1.7 fusion.13
  106.9 2.8 %convolution_bitcast_fusion = f32[4,8,16]{2,0,1:T(4,128)S(1)} fusion(f32[8,16,1296]{2,1,0:T(8,128)S(1)} %fusion.13, f32[4,1296]{1,0:T(4,128)S(1)} %copy-done), kind=kOutput, calls=%fused_computation.13 | convolution fusion | flops 7962624 | bytes 686336 | tf_op jit(solution)/shard_map/yxb,qb->qyx/dot_general | solution.py:129
  111.3 16.8 %all-to-all-start.1 = ((f32[64,1,4,128]{3,2,1,0:T(4,128)}), f32[64,1,4,128]{3,2,1,0:T(4,128)S(1)}, u32[]{:S(2)}, u32[]{:S(2)}) async-start(f32[64,1,4,128]{3,2,1,0:T(4,128)} %fusion.66), calls=%async_computation.1 | async-start | bytes 262144 | tf_op jit(solution)/shard_map/all_to_all | solution.py:136
  128.4 1.9 collective-permute-start.2
  130.4 4.1 %collective-permute-start.3 = (f32[2,8,1,130]{3,2,0,1:T(1,128)S(1)}, f32[2,8,1,130]{3,2,0,1:T(1,128)S(1)}, u32[]{:S(2)}, u32[]{:S(2)}) collective-permute-start(f32[2,8,1,130]{3,2,0,1:T(1,128)S(1)} %get-tuple-element.31), channel_id=1, source_target_pairs={{1,0},{2,1},{3,2},{4,3},{5,4},{6,5},{7,6},{8,7},{9,8},{10,9},{11,1... | collective-permute-start | bytes 24968 | tf_op jit(solution)/shard_map/ppermute | solution.py:29
  134.6 3.5 %collective-permute-done.3 = f32[2,8,1,130]{3,2,0,1:T(1,128)S(1)} collective-permute-done((f32[2,8,1,130]{3,2,0,1:T(1,128)S(1)}, f32[2,8,1,130]{3,2,0,1:T(1,128)S(1)}, u32[]{:S(2)}, u32[]{:S(2)}) %collective-permute-start.3) | collective-permute-done | bytes 8352 | tf_op jit(solution)/shard_map/ppermute | solution.py:29
  138.4 21.6 %all-to-all-done.1 = f32[64,1,4,128]{3,2,1,0:T(4,128)S(1)} async-done(((f32[64,1,4,128]{3,2,1,0:T(4,128)}), f32[64,1,4,128]{3,2,1,0:T(4,128)S(1)}, u32[]{:S(2)}, u32[]{:S(2)}) %all-to-all-start.1) | async-done | bytes 131104 | tf_op jit(solution)/shard_map/all_to_all | solution.py:136
  160.0 2.6 %copy.58 = f32[4,8192]{0,1:T(8,128)} copy(f32[4,8192]{1,0:T(4,128)S(1)} %bitcast.89) | data formatting | bytes 262144 | tf_op jit(solution)/shard_map/reshape | solution.py:137
  162.7 30.0 %gather_fusion.3 = f32[8192,4]{1,0:T(8,128)} fusion(f32[4,8192]{0,1:T(8,128)} %copy.58, s32[8192]{0:T(1024)S(1)} %broadcast_clamp_fusion), kind=kCustom, calls=%fused_computation.3 | custom fusion | bytes 294912 | tf_op jit(solution)/shard_map/gather | solution.py:64
  192.6 2.9 %multiply_reduce_fusion = f32[2048,4]{1,0:T(8,128)S(1)} fusion(f32[4,2048,4]{2,1,0:T(8,128)} %bitcast.87, f32[4,2048]{1,0:T(4,128)S(1)} %bitcast.92), kind=kLoop, calls=%fused_computation.4 | loop fusion | flops 57344 | bytes 196608 | tf_op jit(solution)/shard_map/reduce_sum | solution.py:66
  195.9 2.0 slice_reduce_fusion.3
  (91 shorter events, 23.9 us)
Async XLA Ops:
  0.6 106.3 %copy-start = (f32[4,1296]{1,0:T(4,128)S(1)}, f32[4,1296]{1,0:T(4,128)}, u32[]{:S(2)}) copy-start(f32[4,1296]{1,0:T(4,128)} %param.21) | copy-start | bytes 62212
  1.8 51.1 %collective-permute-start.4 = (f32[8,1,1296]{2,1,0:T(1,128)S(1)}, f32[8,1,1296]{2,1,0:T(1,128)S(1)}, u32[]{:S(2)}, u32[]{:S(2)}) collective-permute-start(f32[8,1,1296]{2,1,0:T(1,128)S(1)} %get-tuple-element.28), channel_id=1, source_target_pairs={{0,16},{16,32},{32,48},{48,64},{64,80},{80,96},{96,112},{112,128},... | collective-permute-start | bytes 124424 | tf_op jit(solution)/shard_map/ppermute | solution.py:26
  3.6 49.4 %collective-permute-start.5 = (f32[8,1,1296]{2,1,0:T(1,128)S(1)}, f32[8,1,1296]{2,1,0:T(1,128)S(1)}, u32[]{:S(2)}, u32[]{:S(2)}) collective-permute-start(f32[8,1,1296]{2,1,0:T(1,128)S(1)} %get-tuple-element.29), channel_id=1, source_target_pairs={{16,0},{32,16},{48,32},{64,48},{80,64},{96,80},{112,96},{128,112},... | collective-permute-start | bytes 124424 | tf_op jit(solution)/shard_map/ppermute | solution.py:29
  9.0 65.2 %all-to-all-start = ((f32[64,2,2,128]{3,2,1,0:T(2,128)}), f32[64,2,2,128]{3,2,1,0:T(2,128)S(1)}, u32[]{:S(2)}, u32[]{:S(2)}) async-start(f32[64,2,2,128]{3,2,1,0:T(2,128)} %broadcast_select_fusion), calls=%async_computation | async-start | bytes 262144 | tf_op jit(solution)/shard_map/all_to_all | solution.py:117
  43.1 85.1 %collective-permute-start = (f32[2,8,16,1]{3,2,0,1:T(8,128)S(1)}, f32[2,8,16,1]{3,2,0,1:T(8,128)S(1)}, u32[]{:S(2)}, u32[]{:S(2)}) collective-permute-start(f32[2,8,16,1]{3,2,0,1:T(8,128)S(1)} %get-tuple-element.38), channel_id=1, source_target_pairs={{0,16},{16,32},{32,48},{48,64},{64,80},{80,96},{96,112},{112,128},... | collective-permute-start | bytes 3080 | tf_op jit(solution)/shard_map/ppermute | solution.py:26
  45.1 83.2 %collective-permute-start.1 = (f32[2,8,16,1]{3,2,0,1:T(8,128)S(1)}, f32[2,8,16,1]{3,2,0,1:T(8,128)S(1)}, u32[]{:S(2)}, u32[]{:S(2)}) collective-permute-start(f32[2,8,16,1]{3,2,0,1:T(8,128)S(1)} %get-tuple-element.39), channel_id=1, source_target_pairs={{16,0},{32,16},{48,32},{64,48},{80,64},{96,80},{112,96},{128,112},... | collective-permute-start | bytes 3080 | tf_op jit(solution)/shard_map/ppermute | solution.py:29
  53.9 30.1 %collective-permute-start.6 = (f32[1,18,1296]{2,1,0:T(8,128)S(1)}, f32[1,18,1296]{2,1,0:T(8,128)S(1)}, u32[]{:S(2)}, u32[]{:S(2)}) collective-permute-start(f32[1,18,1296]{2,1,0:T(8,128)S(1)} %get-tuple-element.24), channel_id=1, source_target_pairs={{0,1},{1,2},{2,3},{3,4},{4,5},{5,6},{6,7},{7,8},{8,9},{9,10},{10,1... | collective-permute-start | bytes 279944 | tf_op jit(solution)/shard_map/ppermute | solution.py:26
  57.0 27.0 %collective-permute-start.7 = (f32[1,18,1296]{2,1,0:T(8,128)S(1)}, f32[1,18,1296]{2,1,0:T(8,128)S(1)}, u32[]{:S(2)}, u32[]{:S(2)}) collective-permute-start(f32[1,18,1296]{2,1,0:T(8,128)S(1)} %get-tuple-element.25), channel_id=1, source_target_pairs={{1,0},{2,1},{3,2},{4,3},{5,4},{6,5},{7,6},{8,7},{9,8},{10,9},{11,1... | collective-permute-start | bytes 279944 | tf_op jit(solution)/shard_map/ppermute | solution.py:29
  74.1 9.9 %copy-start.2 = (f32[8,16,1296]{2,1,0:T(8,128)S(1)}, f32[8,16,1296]{2,1,0:T(8,128)}, u32[]{:S(2)}) copy-start(f32[8,16,1296]{2,1,0:T(8,128)} %param.18) | copy-start | bytes 1990660
  84.0 6.5 %copy-start.8 = (s32[1,1,64,1]{2,3,1,0:T(1,128)S(1)}, s32[1,1,64,1]{2,3,1,0:T(1,128)}, u32[]{:S(2)}) copy-start(s32[1,1,64,1]{2,3,1,0:T(1,128)} %param.25) | copy-start | bytes 772
  84.0 21.3 %copy-start.7 = (bf16[1296,1296]{1,0:T(8,128)(2,1)S(1)}, bf16[1296,1296]{1,0:T(8,128)(2,1)}, u32[]{:S(2)}) copy-start(bf16[1296,1296]{1,0:T(8,128)(2,1)} %param.20) | copy-start | bytes 10077700
  87.9 2.6 %collective-permute-start.8 = (f32[8,1,1296]{2,1,0:T(1,128)S(1)}, f32[8,1,1296]{2,1,0:T(1,128)S(1)}, u32[]{:S(2)}, u32[]{:S(2)}) collective-permute-start(f32[8,1,1296]{2,1,0:T(1,128)S(1)} %get-tuple-element.26), channel_id=1, source_target_pairs={{0,16},{16,32},{32,48},{48,64},{64,80},{80,96},{96,112},{112,128},... | collective-permute-start | bytes 124424 | tf_op jit(solution)/shard_map/ppermute | solution.py:26
  89.2 3.9 %collective-permute-start.9 = (f32[8,1,1296]{2,1,0:T(1,128)S(1)}, f32[8,1,1296]{2,1,0:T(1,128)S(1)}, u32[]{:S(2)}, u32[]{:S(2)}) collective-permute-start(f32[8,1,1296]{2,1,0:T(1,128)S(1)} %get-tuple-element.27), channel_id=1, source_target_pairs={{16,0},{32,16},{48,32},{64,48},{80,64},{96,80},{112,96},{128,112},... | collective-permute-start | bytes 124424 | tf_op jit(solution)/shard_map/ppermute | solution.py:29
  93.2 6.9 %collective-permute-start.10 = (f32[1,18,1296]{2,1,0:T(8,128)S(1)}, f32[1,18,1296]{2,1,0:T(8,128)S(1)}, u32[]{:S(2)}, u32[]{:S(2)}) collective-permute-start(f32[1,18,1296]{2,1,0:T(8,128)S(1)} %get-tuple-element.22), channel_id=1, source_target_pairs={{0,1},{1,2},{2,3},{3,4},{4,5},{5,6},{6,7},{7,8},{8,9},{9,10},{10,1... | collective-permute-start | bytes 279944 | tf_op jit(solution)/shard_map/ppermute | solution.py:26
  96.2 9.0 %collective-permute-start.11 = (f32[1,18,1296]{2,1,0:T(8,128)S(1)}, f32[1,18,1296]{2,1,0:T(8,128)S(1)}, u32[]{:S(2)}, u32[]{:S(2)}) collective-permute-start(f32[1,18,1296]{2,1,0:T(8,128)S(1)} %get-tuple-element.23), channel_id=1, source_target_pairs={{1,0},{2,1},{3,2},{4,3},{5,4},{6,5},{7,6},{8,7},{9,8},{10,9},{11,1... | collective-permute-start | bytes 279944 | tf_op jit(solution)/shard_map/ppermute | solution.py:29
  99.0 29.2 %copy-start.1 = (f32[2,8,16,128]{3,2,1,0:T(8,128)S(1)}, f32[2,8,16,128]{3,2,1,0:T(8,128)}, u32[]{:S(2)}) copy-start(f32[2,8,16,128]{3,2,1,0:T(8,128)} %param.15) | copy-start | bytes 393220
  99.0 29.2 %copy-start.4 = (s32[4,16,128]{2,1,0:T(8,128)S(1)}, s32[4,16,128]{2,1,0:T(8,128)}, u32[]{:S(2)}) copy-start(s32[4,16,128]{2,1,0:T(8,128)} %param.27) | copy-start | bytes 98308
  99.1 35.5 %copy-start.5 = (s32[16,128]{1,0:T(8,128)S(1)}, s32[16,128]{1,0:T(8,128)}, u32[]{:S(2)}) copy-start(s32[16,128]{1,0:T(8,128)} %param.16) | copy-start | bytes 24580
  106.9 85.7 %copy-start.3 = (f32[8,16,1296]{2,1,0:T(8,128)}, f32[8,16,1296]{2,1,0:T(8,128)S(1)}, u32[]{:S(2)}) copy-start(f32[8,16,1296]{2,1,0:T(8,128)S(1)} %fusion.13) | copy-start | bytes 1990660
  111.3 48.7 %all-to-all-start.1 = ((f32[64,1,4,128]{3,2,1,0:T(4,128)}), f32[64,1,4,128]{3,2,1,0:T(4,128)S(1)}, u32[]{:S(2)}, u32[]{:S(2)}) async-start(f32[64,1,4,128]{3,2,1,0:T(4,128)} %fusion.66), calls=%async_computation.1 | async-start | bytes 262144 | tf_op jit(solution)/shard_map/all_to_all | solution.py:136
  128.4 6.1 %collective-permute-start.2 = (f32[2,8,1,130]{3,2,0,1:T(1,128)S(1)}, f32[2,8,1,130]{3,2,0,1:T(1,128)S(1)}, u32[]{:S(2)}, u32[]{:S(2)}) collective-permute-start(f32[2,8,1,130]{3,2,0,1:T(1,128)S(1)} %get-tuple-element.30), channel_id=1, source_target_pairs={{0,1},{1,2},{2,3},{3,4},{4,5},{5,6},{6,7},{7,8},{8,9},{9,10},{10,1... | collective-permute-start | bytes 24968 | tf_op jit(solution)/shard_map/ppermute | solution.py:26
  130.4 7.7 %collective-permute-start.3 = (f32[2,8,1,130]{3,2,0,1:T(1,128)S(1)}, f32[2,8,1,130]{3,2,0,1:T(1,128)S(1)}, u32[]{:S(2)}, u32[]{:S(2)}) collective-permute-start(f32[2,8,1,130]{3,2,0,1:T(1,128)S(1)} %get-tuple-element.31), channel_id=1, source_target_pairs={{1,0},{2,1},{3,2},{4,3},{5,4},{6,5},{7,6},{8,7},{9,8},{10,9},{11,1... | collective-permute-start | bytes 24968 | tf_op jit(solution)/shard_map/ppermute | solution.py:29
  195.5 2.4 %copy-start.6 = (f32[16]{0:T(128)S(1)}, f32[16]{0:T(128)}, u32[]{:S(2)}) copy-start(f32[16]{0:T(128)} %param.17) | copy-start | bytes 196
where the time goes:
time: 200 us; the launch traced here: 199 us
  starting transfers between devices  76.5 us (38%)
  local copies, waits for them, and re-layouts  51.8 us (26%)
  waiting for transfers between devices  48.3 us (24%)
  other arithmetic  12.7 us (6%)
  matrix products  8.27 us (4%)
    gather x2, local copies, waits for them, and re-layouts, weighted_pick(): values = buffer[:, index]  34.4 us
    all_to_all x1, starting transfers between devices, on_device(): lax.all_to_all(outgoing, 'tile', split_axis=0, concat_axis=0, tiled=True)  33.1 us
    all_to_all x1, waiting for transfers between devices, on_device(): lax.all_to_all(returning, 'tile', split_axis=0, concat_axis=0, tiled=True)  21.6 us
    all_to_all x1, starting transfers between devices, on_device(): lax.all_to_all(returning, 'tile', split_axis=0, concat_axis=0, tiled=True)  16.8 us
    all_to_all x1, waiting for transfers between devices, on_device(): lax.all_to_all(outgoing, 'tile', split_axis=0, concat_axis=0, tiled=True)  14.3 us
    ppermute x6, starting transfers between devices, with_halo(): lax.ppermute(lax.slice_in_dim(block, 0, width, axis=dim), axis, backward)  13.5 us
    ppermute x6, starting transfers between devices, with_halo(): lax.ppermute(lax.slice_in_dim(block, block.shape[dim] - width, None, axis...  13 us
    ppermute x6, waiting for transfers between devices, with_halo(): lax.ppermute(lax.slice_in_dim(block, 0, width, axis=dim), axis, backward)  11.3 us
  transfers between devices with their start and end apart: 14, of which 6 were waited for; matrix products, arithmetic and copies ran while one was open for 17% of the time, Pallas kernels for 0%

commit v1 on v0

v1 whole, which is shorter than its diff:
```python
import functools
import math

import jax
import jax.numpy as jnp
import numpy as np
from jax import lax
from jax.experimental import pallas as pl
from jax.experimental.pallas import tpu as pltpu
from jax.sharding import PartitionSpec as P

NDIR = 36
NFREQ = 36
DT_OCEAN = 0.2
VISCOSITY = 0.5
VERT_FRICTION = 0.5
STRESS_COEFF = 1.0
DT_WAVE = 0.1
DT_SOURCE = 0.3

LANES = 128
MESH = pl.DeviceIdType.MESH
HIGHEST = lax.Precision.HIGHEST


def chunks(total, size):
    return [(start, min(start + size, total)) for start in range(0, total, size)]


def lane_pick(table, index):
    return jnp.take_along_axis(table, index, axis=1, mode="promise_in_bounds")


def kernel(
    tiles,
    bands,
    group,
    ocean_h, wet_h, coriolis_h, spectrum_h, speed_h, source_h, moments_h,
    o2w_rows_h, o2w_index_h, o2w_weight_h, w2o_rows_h, w2o_index_h, w2o_weight_h,
    wheel_h, wheel_index_h,
    ocean_out, spectrum_out,
    ocean, wet, coriolis, first, speed, source, moments,
    o2w_rows, o2w_index, o2w_weight, w2o_index, w2o_weight, wheel, wheel_index,
    outgoing, incoming, marks, totals,
    edge_w0, edge_e0, halo_w0, halo_e0, edge_w1, edge_e1, halo_w1, halo_e1,
    row_lo, row_hi, halo_lo, halo_hi, column_w, column_e, arrived_w, arrived_e,
    second, moved, rounded, leftover, speed_x, speed_y, flow_x, flow_y,
    halo_column, pad_small, pad_rows, pad_index, pad_moments, moments_t, mixed_t, mark_lanes,
    ocean_new, spectrum_new,
    load_sem, send_sem, recv_sem,
):
    tile, band = lax.axis_index("tile"), lax.axis_index("band")
    groups = tiles // group
    my_group, my_place = tile // group, tile % group
    east, west = lax.rem(tile + 1, tiles), lax.rem(tile + tiles - 1, tiles)
    north, south = lax.rem(band + 1, bands), lax.rem(band + bands - 1, bands)
    bins = first.shape[2]
    layers = ocean.shape[0]
    levels = layers // 2

    loads = [
        (ocean_h, ocean.at[:, 8:24, :]), (o2w_rows_h, o2w_rows), (spectrum_h, first.at[1:9, 8:24, :]),
        (w2o_rows_h, marks.at[my_place * groups + my_group]), (moments_h, moments), (source_h, source),
        (o2w_index_h, o2w_index), (o2w_weight_h, o2w_weight), (speed_h, speed), (wheel_h, wheel),
        (wheel_index_h, wheel_index), (wet_h, wet), (coriolis_h, coriolis), (w2o_index_h, w2o_index),
        (w2o_weight_h, w2o_weight),
    ]
    loads = [pltpu.make_async_copy(s, d, load_sem.at[i]) for i, (s, d) in enumerate(loads)]
    for load in loads:
        load.start()

    barrier = pltpu.get_barrier_semaphore()

    def greet(step, carry):
        pl.semaphore_signal(
            barrier, inc=1, device_id={"tile": lax.rem(tile + step, tiles)}, device_id_type=MESH
        )
        return carry

    lax.fori_loop(1, tiles, greet, 0)
    for other in (south, north):
        pl.semaphore_signal(barrier, inc=1, device_id={"band": other}, device_id_type=MESH)

    loads[0].wait()
    loads[1].wait()
    pad_rows[...] = jnp.zeros_like(pad_rows)
    pad_rows[0:2, 0:tiles] = o2w_rows[...]
    wanted = jnp.transpose(pad_rows[...].astype(jnp.float32))
    for slot in range(2):
        row = jnp.broadcast_to(wanted[0:tiles, slot : slot + 1], (tiles, LANES))
        east_part = jnp.zeros((tiles, LANES), jnp.float32)
        north_part = east_part
        for r in range(16):
            here = row == float(r)
            east_part = jnp.where(here, ocean[0, 8 + r : 9 + r, :], east_part)
            north_part = jnp.where(here, ocean[levels, 8 + r : 9 + r, :], north_part)
        outgoing[:, 2 * slot, :] = east_part
        outgoing[:, 2 * slot + 1, :] = north_part
    pl.semaphore_wait(barrier, tiles + 1)

    keep = pltpu.make_async_copy(outgoing.at[tile], incoming.at[tile], recv_sem.at[0])
    keep.start()

    def give(step, carry):
        half = (step + 1) // 2
        reach = tiles // 2 + half * (1 - 2 * (step % 2))
        target = lax.rem(tile + reach, tiles)
        pltpu.make_async_remote_copy(
            src_ref=outgoing.at[target], dst_ref=incoming.at[tile], send_sem=send_sem.at[0],
            recv_sem=recv_sem.at[0], device_id={"tile": target}, device_id_type=MESH,
        ).start()
        return carry

    lax.fori_loop(0, tiles - 1, give, 0)

    def send(index, src, dst, where):
        copy = pltpu.make_async_remote_copy(
            src_ref=src, dst_ref=dst, send_sem=send_sem.at[index], recv_sem=recv_sem.at[index],
            device_id=where, device_id_type=MESH,
        )
        copy.start()
        return copy

    def spread_far(index, ref):
        own = my_place * groups + my_group
        for step in range(1, groups):
            target = lax.rem(my_group + step, groups) * group + my_place
            send(index, ref.at[own], ref.at[own], {"tile": target})

    def spread_near(index, ref):
        own = pl.ds(my_place * groups, groups)
        for step in range(1, group):
            target = my_group * group + lax.rem(my_place + step, group)
            send(index, ref.at[own], ref.at[own], {"tile": target})

    def await_blocks(sem, ref, count):
        part = ref.at[pl.ds(0, count)]
        pltpu.make_async_copy(part, part, sem).wait()

    def send_edges(base, field, edge_w, edge_e, halo_w, halo_e):
        edge_w[...] = field[1:9, 8, :]
        edge_e[...] = field[1:9, 23, :]
        return [
            send(base, field.at[1, 8:24, :], field.at[9, 8:24, :], {"band": south}),
            send(base + 1, field.at[8, 8:24, :], field.at[0, 8:24, :], {"band": north}),
            send(base + 2, edge_w, halo_e, {"tile": west}),
            send(base + 3, edge_e, halo_w, {"tile": east}),
        ]

    def place_edges(copies, field, halo_w, halo_e):
        for copy in copies:
            copy.wait_recv()
        field[1:9, 7, :] = halo_w[...] * jnp.where(tile == 0, 0.0, 1.0)
        field[1:9, 24, :] = halo_e[...] * jnp.where(tile == tiles - 1, 0.0, 1.0)

        @pl.when(band == 0)
        def _():
            field[0, 8:24, :] = jnp.zeros((16, bins), jnp.float32)

        @pl.when(band == bands - 1)
        def _():
            field[9, 8:24, :] = jnp.zeros((16, bins), jnp.float32)

    loads[2].wait()
    edges = send_edges(1, first, edge_w0, edge_e0, halo_w0, halo_e0)
    loads[3].wait()
    spread_far(5, marks)

    row_lo[...] = ocean[:, 8, :]
    row_hi[...] = ocean[:, 23, :]
    flat = ocean[:, 8:24, :].reshape(layers * 16, LANES)
    turned = jnp.transpose(flat)
    column_w[...] = jnp.broadcast_to(turned[0:1, :], column_w.shape)
    column_e[...] = jnp.broadcast_to(turned[LANES - 1 : LANES, :], column_e.shape)
    ocean_edges = [
        send(7, row_lo, halo_hi, {"band": south}),
        send(8, row_hi, halo_lo, {"band": north}),
    ]
    ocean_edges += [
        send(9, column_w, arrived_e, {"tile": west}),
        send(10, column_e, arrived_w, {"tile": east}),
    ]

    for load in (4, 8, 9, 10):
        loads[load].wait()
    pad_small[...] = jnp.zeros_like(pad_small)
    pad_small[0:1, 0:NFREQ] = speed[...]
    speeds = jnp.broadcast_to(pad_small[0:1, :], (8, LANES))
    for lo, hi in chunks(speed_x.shape[1], LANES):
        picked = lane_pick(speeds, wheel_index[:, lo:hi])
        speed_x[:, lo:hi] = picked * wheel[0:1, lo:hi]
        speed_y[:, lo:hi] = picked * wheel[1:2, lo:hi]

    pad_moments[...] = jnp.zeros_like(pad_moments)
    pad_moments[0:4, 0:bins] = moments[...]
    for lo, hi in chunks(pad_moments.shape[1], LANES):
        top = min(hi, bins)
        part = jnp.transpose(pad_moments[:, lo:hi])
        high = part.astype(jnp.bfloat16)
        low = part - high.astype(jnp.float32)
        both = high.astype(jnp.float32) + pltpu.roll(low, 8, 1)
        moments_t[lo:top, :] = both[0 : top - lo].astype(jnp.bfloat16)
    loads[5].wait()
    lane = lax.broadcasted_iota(jnp.int32, (144, LANES), 1)

    def mix(step, carry):
        rows = pl.ds(pl.multiple_of(step * 144, 144), 144)
        mixed = jnp.dot(source[rows, :], moments_t[...], preferred_element_type=jnp.float32)
        own = moments_t[rows, :].astype(jnp.float32)
        full = own + DT_SOURCE * mixed
        full = jnp.where(lane < 8, full + pltpu.roll(full, LANES - 8, 1), 0.0)
        high = full.astype(jnp.bfloat16)
        low = full - high.astype(jnp.float32)
        both = high.astype(jnp.float32) + pltpu.roll(low, 8, 1)
        mixed_t[rows, :] = both.astype(jnp.bfloat16)
        return carry

    lax.fori_loop(0, bins // 144, mix, 0)

    await_blocks(recv_sem.at[5], marks, groups - 1)
    spread_near(6, marks)

    for copy in ocean_edges:
        copy.wait_recv()
    loads[11].wait()
    loads[12].wait()
    ocean[:, 7, :] = halo_lo[...] * jnp.where(band == 0, 0.0, 1.0)
    ocean[:, 24, :] = halo_hi[...] * jnp.where(band == bands - 1, 0.0, 1.0)
    halo_column[...] = jnp.zeros_like(halo_column)
    halo_column[0, 0:8, :] = arrived_w[...]
    halo_column[1, LANES - 8 : LANES, :] = arrived_e[...]
    column_from_w = jnp.transpose(halo_column[0]) * jnp.where(tile == 0, 0.0, 1.0)
    column_from_e = jnp.transpose(halo_column[1]) * jnp.where(tile == tiles - 1, 0.0, 1.0)
    spot = lax.broadcasted_iota(jnp.int32, (16, LANES), 1)
    line = lax.broadcasted_iota(jnp.int32, (16, LANES), 0)
    pad_small[...] = jnp.zeros_like(pad_small)
    pad_small[0:1, 0:16] = coriolis[...]
    rotation = jnp.sum(
        jnp.where(spot == line, jnp.broadcast_to(pad_small[0:1, :], (16, LANES)), 0.0),
        axis=1, keepdims=True,
    )
    rotation = jnp.broadcast_to(rotation, (16, LANES))
    wet_now = wet[...].astype(jnp.float32)
    for level in range(levels):
        for part in range(2):
            n = part * levels + level
            here = ocean[n, 8:24, :]
            lanes_w = jnp.where(spot == 0, column_from_w[16 * n : 16 * n + 16], pltpu.roll(here, 1, 1))
            lanes_e = jnp.where(
                spot == LANES - 1, column_from_e[16 * n : 16 * n + 16], pltpu.roll(here, LANES - 1, 1)
            )
            laplace = ocean[n, 7:23, :] + ocean[n, 9:25, :] + lanes_w + lanes_e - 4.0 * here
            above = ocean[n - 1 if level > 0 else n, 8:24, :]
            below = ocean[n + 1 if level < levels - 1 else n, 8:24, :]
            vertical = above - 2.0 * here + below
            if part == 0:
                turning = rotation * ocean[n + levels, 8:24, :]
            else:
                turning = -rotation * ocean[n - levels, 8:24, :]
            tendency = VISCOSITY * laplace + VERT_FRICTION * vertical + turning
            ocean_new[n] = wet_now * (here + DT_OCEAN * tendency)

    await_blocks(recv_sem.at[6], marks, (group - 1) * groups)
    mark = jnp.where(marks[:, 0, :] < 1, 1.0, 0.0)
    column = lax.broadcasted_iota(jnp.int32, (8, tiles), 1)
    mine = jnp.where(column == tile, 1.0, 0.0)
    mark_lanes[...] = jnp.zeros_like(mark_lanes)
    mark_lanes[:, 0:tiles] = lax.dot_general(mine, mark, (((1,), (1,)), ((), ())))

    loads[6].wait()
    loads[7].wait()
    spot8 = lax.broadcasted_iota(jnp.int32, (8, LANES), 1)
    pad_index[...] = jnp.zeros_like(pad_index)
    pad_index[0:4, :, 0:16] = o2w_index[...]
    pad_index[4:8, :, 0:16] = o2w_weight[...]
    index, weight = pad_index[0], pad_index[4]
    for k in range(1, 4):
        index = index + pltpu.roll(pad_index[k], 16 * k, 1)
        weight = weight + pltpu.roll(pad_index[4 + k], 16 * k, 1)
    index = index + pltpu.roll(index, 64, 1)
    weight = (weight + pltpu.roll(weight, 64, 1)).astype(jnp.float32)
    code, spot_index = index >> 7, index & 127
    is_east = spot8 < 64

    place_edges(edges, first, halo_w0, halo_e0)
    pltpu.make_async_copy(incoming, incoming, recv_sem.at[0]).wait()

    def pick_current(step, picked):
        for inner in range(4):
            block = step * 4 + inner
            for slot in range(2):
                a = lane_pick(jnp.broadcast_to(incoming[block, 2 * slot : 2 * slot + 1, :], (8, LANES)), spot_index)
                c = lane_pick(jnp.broadcast_to(incoming[block, 2 * slot + 1 : 2 * slot + 2, :], (8, LANES)), spot_index)
                picked = jnp.where(code == block * 2 + slot, jnp.where(is_east, a, c), picked)
        return picked

    picked = lax.fori_loop(0, tiles // 4, pick_current, jnp.zeros((8, LANES), jnp.float32))
    weighted = picked * weight
    weighted = weighted + pltpu.roll(weighted, LANES - 16, 1)
    weighted = weighted + pltpu.roll(weighted, LANES - 32, 1)
    weight = weight + pltpu.roll(weight, LANES - 16, 1)
    weight = weight + pltpu.roll(weight, LANES - 32, 1)
    currents = jnp.transpose(weighted / weight)
    for y in range(8):
        flow_x[y] = jnp.broadcast_to(currents[0:16, y : y + 1], (16, LANES))
        flow_y[y] = jnp.broadcast_to(currents[64:80, y : y + 1], (16, LANES))

    def advect(field, last):
        def one_row(y, carry):
            rows = pl.ds(pl.multiple_of(y * 16, 16), 16)
            current_x, current_y = flow_x[y], flow_y[y]
            for lo, hi in chunks(bins, LANES):
                center = field[y + 1, 8:24, lo:hi]
                flow = speed_x[0:1, lo:hi] + current_x[:, : hi - lo]
                change = flow * jnp.where(
                    flow > 0.0, center - field[y + 1, 7:23, lo:hi], field[y + 1, 9:25, lo:hi] - center
                )
                flow = speed_y[0:1, lo:hi] + current_y[:, : hi - lo]
                change += flow * jnp.where(
                    flow > 0.0, center - field[y, 8:24, lo:hi], field[y + 2, 8:24, lo:hi] - center
                )
                result = center - DT_WAVE * change
                moved[rows, lo:hi] = result
                coarse = result.astype(jnp.bfloat16)
                rounded[rows, lo:hi] = coarse
                if last:
                    leftover[rows, lo:hi] = (result - coarse.astype(jnp.float32)).astype(jnp.bfloat16)
            return carry

        lax.fori_loop(0, 8, one_row, 0)

    def react(lo, hi):
        product = jnp.dot(rounded[...], source[:, lo:hi], preferred_element_type=jnp.float32)
        return (moved[:, lo:hi] + DT_SOURCE * product).reshape(8, 16, hi - lo)

    advect(first, False)
    for lo, hi in chunks(bins, 256):
        second[1:9, 8:24, lo:hi] = react(lo, hi)
    edges2 = send_edges(11, second, edge_w1, edge_e1, halo_w1, halo_e1)
    place_edges(edges2, second, halo_w1, halo_e1)
    advect(second, True)
    sums = jnp.dot(rounded[...], mixed_t[...], preferred_element_type=jnp.float32)
    sums += jnp.dot(leftover[...], moments_t[...], preferred_element_type=jnp.float32)
    sums = jnp.transpose(sums + pltpu.roll(sums, LANES - 8, 1))
    totals[my_place * groups + my_group] = sums[0:4, :]
    spread_far(15, totals)
    parts = chunks(bins, 256)
    for lo, hi in parts[:3]:
        spectrum_new[:, :, lo:hi] = react(lo, hi)
    await_blocks(recv_sem.at[15], totals, groups - 1)
    spread_near(16, totals)
    for lo, hi in parts[3:]:
        spectrum_new[:, :, lo:hi] = react(lo, hi)
    store_spectrum = pltpu.make_async_copy(spectrum_new, spectrum_out, load_sem.at[15])
    store_spectrum.start()

    loads[13].wait()
    loads[14].wait()
    await_blocks(recv_sem.at[16], totals, (group - 1) * groups)
    marked = mark_lanes[...]
    for half in range(2):
        rows = slice(8 * half, 8 * half + 8)
        spots, codes, factors = [], [], []
        share = jnp.zeros((8, LANES), jnp.float32)
        for k in range(4):
            entry = w2o_index[k, rows, :]
            block = entry >> 7
            block = (block & (group - 1)) * groups + (block >> (group.bit_length() - 1))
            factor = w2o_weight[k, rows, :].astype(jnp.float32)
            share = share + factor
            spots.append(entry & 127)
            codes.append(block)
            factors.append(factor * lane_pick(marked, block))

        def pick_total(step, carry):
            carry = list(carry)
            for inner in range(2):
                block = step * 2 + inner
                tables = [jnp.broadcast_to(totals[block, q : q + 1, :], (8, LANES)) for q in range(4)]
                for k in range(4):
                    here = codes[k] == block
                    for q in range(4):
                        carry[4 * k + q] = jnp.where(here, lane_pick(tables[q], spots[k]), carry[4 * k + q])
            return tuple(carry)

        found = lax.fori_loop(
            0, tiles // 2, pick_total, tuple(jnp.zeros((8, LANES), jnp.float32) for _ in range(16))
        )
        forcing = []
        for q in range(4):
            total = factors[0] * found[q]
            for k in range(1, 4):
                total = total + factors[k] * found[4 * k + q]
            forcing.append(total / share)
        turn = rotation[rows]
        scale = wet_now[rows] * DT_OCEAN
        ocean_new[0, rows, :] += scale * (STRESS_COEFF * forcing[0] + turn * forcing[3])
        ocean_new[levels, rows, :] += scale * (STRESS_COEFF * forcing[1] - turn * forcing[2])
    store_ocean = pltpu.make_async_copy(ocean_new, ocean_out, load_sem.at[16])
    store_ocean.start()

    for copy in edges + ocean_edges + edges2:
        copy.wait_send()
    await_blocks(send_sem.at[0], outgoing, tiles - 1)
    for index, ref in ((5, marks), (15, totals)):
        await_blocks(send_sem.at[index], ref, groups - 1)
        await_blocks(send_sem.at[index + 1], ref, (group - 1) * groups)
    store_spectrum.wait()
    store_ocean.wait()


def on_device(
    tiles,
    bands,
    ocean_velocity,
    ocean_wet,
    coriolis,
    spectrum,
    group_speed,
    source_matrix,
    moments,
    o2w_rows,
    ocean_to_wave_index,
    o2w_weight,
    w2o_rows,
    wave_to_ocean_index,
    wave_to_ocean_weight,
):
    components, levels, rows, columns = ocean_velocity.shape
    layers = components * levels
    height, width, bins = spectrum.shape
    padded_bins = -(-bins // LANES) * LANES
    group = 1 << (max(tiles.bit_length() - 1, 2) // 2)
    angle = (np.arange(NDIR) + 0.5) * (2.0 * math.pi / NDIR)
    wheel = np.zeros((8, padded_bins), np.float32)
    wheel[0, :bins] = np.repeat(np.cos(angle), NFREQ)
    wheel[1, :bins] = np.repeat(np.sin(angle), NFREQ)
    wheel_index = np.zeros((8, padded_bins), np.int32)
    wheel_index[:, :bins] = np.tile(np.arange(NFREQ), NDIR)
    operands = (
        ocean_velocity.reshape(layers, rows, columns),
        ocean_wet,
        coriolis.reshape(1, rows),
        spectrum,
        group_speed.reshape(1, NFREQ),
        source_matrix,
        moments,
        o2w_rows[0, 0].T,
        ocean_to_wave_index,
        o2w_weight,
        w2o_rows[0, 0].T,
        wave_to_ocean_index,
        wave_to_ocean_weight,
        jnp.asarray(wheel),
        jnp.asarray(wheel_index),
    )
    f32, bf16, i32 = jnp.float32, jnp.bfloat16, jnp.int32
    V = pltpu.VMEM
    scratch = [
        V((layers, 32, columns), f32), V((rows, columns), i32), V((1, rows), f32), V((10, 32, bins), f32),
        V((1, NFREQ), f32), V((bins, bins), bf16), V((4, bins), f32),
        V((2, tiles), i32), V((4, height, width), i32), V((4, height, width), i32),
        V((4, rows, columns), i32), V((4, rows, columns), i32), V((8, padded_bins), f32), V((8, padded_bins), i32),
        V((tiles, 4, LANES), f32), V((tiles, 4, LANES), f32), V((tiles, 1, tiles), i32), V((tiles, 4, LANES), f32),
    ]
    scratch += [V((height, bins), f32)] * 8
    scratch += [V((layers, columns), f32)] * 4
    scratch += [V((8, layers * rows), f32)] * 4
    scratch += [
        V((10, 32, bins), f32), V((LANES, bins), f32), V((LANES, bins), bf16), V((LANES, bins), bf16),
        V((8, padded_bins), f32), V((8, padded_bins), f32), V((height, 16, LANES), f32), V((height, 16, LANES), f32),
        V((2, LANES, layers * rows), f32), V((8, LANES), f32), V((LANES, LANES), i32), V((8, height, LANES), i32), V((LANES, padded_bins), f32),
        V((bins, LANES), bf16), V((bins, LANES), bf16), V((8, LANES), f32),
        V((layers, rows, columns), f32), V((height, width, bins), f32),
        pltpu.SemaphoreType.DMA((17,)), pltpu.SemaphoreType.DMA((17,)), pltpu.SemaphoreType.DMA((17,)),
    ]
    any_space = pl.BlockSpec(memory_space=pl.ANY)
    ocean_next, spectrum_next = pl.pallas_call(
        functools.partial(kernel, tiles, bands, group),
        out_shape=(
            jax.ShapeDtypeStruct((layers, rows, columns), f32),
            jax.ShapeDtypeStruct((height, width, bins), f32),
        ),
        in_specs=[any_space] * len(operands),
        out_specs=(any_space, any_space),
        scratch_shapes=scratch,
        compiler_params=pltpu.CompilerParams(
            collective_id=0, has_side_effects=True, vmem_limit_bytes=48 << 20
        ),
        name="coupled_step",
    )(*operands)
    return ocean_next.reshape(ocean_velocity.shape), spectrum_next


def solution(mesh):
    placed = (
        P(None, None, "band", "tile"),
        P("band", "tile"),
        P("band"),
        P("band", "tile", None),
        P(),
        P(),
        P(),
        P("tile", "band", None, None),
        P(None, "band", "tile"),
        P(None, "band", "tile"),
        P("tile", "band", None, None),
        P(None, "band", "tile"),
        P(None, "band", "tile"),
    )
    return jax.shard_map(
        functools.partial(on_device, mesh.shape["tile"], mesh.shape["band"]),
        mesh=mesh,
        in_specs=placed,
        out_specs=(P(None, None, "band", "tile"), P("band", "tile", None)),
        check_vma=False,
    )
```

time: 200 us -> 109 us (0.55)
  the two profiles are of different devices: /device:TPU:24 before, /device:TPU:1 now
where the time goes in v1:
time: 109 us; the launch traced here: 108 us
  Pallas kernels  93.6 us (86%)
  local copies, waits for them, and re-layouts  14.1 us (13%)
    pallas_call x1, Pallas kernels, on_device(): pl.pallas_call(functools.partial(kernel, tiles, bands, group), out_shape=...  93.6 us
    unnamed x32, local copies, waits for them, and re-layouts  14.1 us

profile of v1, /device:TPU:1, one launch (start us, length us, event | category | flops | bytes accessed | tf_op | source)
XLA Modules:
  0.0 108.4 jit_solution(2111810040176562838)
XLA Ops:
  0.6 0.0 copy-start
  0.6 2.0 %copy-done = bf16[1296,1296]{1,0:T(8,128)(2,1)S(1)} copy-done((bf16[1296,1296]{1,0:T(8,128)(2,1)S(1)}, bf16[1296,1296]{1,0:T(8,128)(2,1)}, u32[]{:S(2)}) %copy-start) | copy-done | bytes 3359256
  2.7 0.0 copy-start.1
  2.7 1.1 %copy-done.1 = f32[8,16,1296]{2,1,0:T(8,128)S(1)} copy-done((f32[8,16,1296]{2,1,0:T(8,128)S(1)}, f32[8,16,1296]{2,1,0:T(8,128)}, u32[]{:S(2)}) %copy-start.1) | copy-done | bytes 663576
  3.8 0.0 copy-start.2
  3.8 0.9 copy-done.2
  4.7 0.0 copy-start.3
  4.7 0.8 copy-done.3
  5.5 0.0 copy-start.4
  5.5 0.8 copy-done.4
  6.3 0.0 copy-start.5
  6.3 0.8 copy-done.5
  7.0 0.8 copy-done.6
  7.8 0.7 copy-done.7
  8.5 0.7 copy-done.8
  9.2 0.7 copy-done.9
  9.9 0.7 copy-done.10
  10.6 0.7 copy-done.11
  11.3 0.7 copy-done.12
  12.0 0.7 copy-done.13
  12.6 0.7 copy-done.14
  13.3 93.6 %coupled_step.1 = (f32[16,16,128]{2,1,0:T(8,128)S(1)}, f32[8,16,1296]{2,1,0:T(8,128)S(1)}) custom-call(f32[16,16,128]{2,1,0:T(8,128)S(1)} %bitcast.8, s32[16,128]{1,0:T(8,128)S(1)} %copy-done.10, f32[1,16]{1,0:T(1,128)S(1)} %bitcast.11, f32[8,16,1296]{2,1,0:T(8,128)S(1)} %copy-done.1, f32[1,36]{1,0:T(1,128)S(1)} %bitcast.12, bf16[1296,1296]{1,0:T(8,128)(2,1)S(1)} %copy-done, ...), custom_call_target="tpu_custom_call" | custom-call | tf_op jit(solution)/shard_map/coupled_step/pallas_call | solution.py:478
  106.9 0.7 copy.19
  107.6 0.9 copy.20
  (9 shorter events, 0.0 us)
Async XLA Ops:
  0.6 2.0 %copy-start = (bf16[1296,1296]{1,0:T(8,128)(2,1)S(1)}, bf16[1296,1296]{1,0:T(8,128)(2,1)}, u32[]{:S(2)}) copy-start(bf16[1296,1296]{1,0:T(8,128)(2,1)} %source_h.1) | copy-start | bytes 10077700
  2.7 1.1 %copy-start.1 = (f32[8,16,1296]{2,1,0:T(8,128)S(1)}, f32[8,16,1296]{2,1,0:T(8,128)}, u32[]{:S(2)}) copy-start(f32[8,16,1296]{2,1,0:T(8,128)} %spectrum_h.1) | copy-start | bytes 1990660
  3.8 0.9 copy-start.2
  4.7 0.8 copy-start.3
  5.5 0.8 copy-start.4
  6.3 0.8 copy-start.5
  7.0 0.8 copy-start.6
  7.8 0.7 copy-start.7
  8.5 0.7 copy-start.8
  9.2 0.7 copy-start.9
  9.9 0.7 copy-start.10
  10.6 0.7 copy-start.11
  11.3 0.7 copy-start.12
  12.0 0.7 copy-start.13
  12.6 0.7 copy-start.14

commit v2 on v1

--- a/solution.py
+++ b/solution.py
@@ -34,33 +34,45 @@
 def kernel(
     tiles,
     bands,
-    group,
     ocean_h, wet_h, coriolis_h, spectrum_h, speed_h, source_h, moments_h,
     o2w_rows_h, o2w_index_h, o2w_weight_h, w2o_rows_h, w2o_index_h, w2o_weight_h,
     wheel_h, wheel_index_h,
     ocean_out, spectrum_out,
     ocean, wet, coriolis, first, speed, source, moments,
-    o2w_rows, o2w_index, o2w_weight, w2o_index, w2o_weight, wheel, wheel_index,
-    outgoing, incoming, marks, totals,
+    o2w_rows, w2o_rows, o2w_index, o2w_weight, w2o_index, w2o_weight, wheel, wheel_index,
+    outgoing, incoming, marks, totals, arrived,
     edge_w0, edge_e0, halo_w0, halo_e0, edge_w1, edge_e1, halo_w1, halo_e1,
     row_lo, row_hi, halo_lo, halo_hi, column_w, column_e, arrived_w, arrived_e,
     second, moved, rounded, leftover, speed_x, speed_y, flow_x, flow_y,
-    halo_column, pad_small, pad_rows, pad_index, pad_moments, moments_t, mixed_t, mark_lanes,
-    ocean_new, spectrum_new,
+    halo_column, pad_small, pad_rows, pad_index, pad_moments, moments_t, mixed_t,
     load_sem, send_sem, recv_sem,
 ):
     tile, band = lax.axis_index("tile"), lax.axis_index("band")
-    groups = tiles // group
-    my_group, my_place = tile // group, tile % group
     east, west = lax.rem(tile + 1, tiles), lax.rem(tile + tiles - 1, tiles)
     north, south = lax.rem(band + 1, bands), lax.rem(band + bands - 1, bands)
     bins = first.shape[2]
     layers = ocean.shape[0]
     levels = layers // 2
 
+    def far_first(step):
+        half = (step + 1) // 2
+        return lax.rem(tile + tiles // 2 + half * (1 - 2 * (step % 2)), tiles)
+
+    barrier = pltpu.get_barrier_semaphore()
+
+    def greet(step, carry):
+        pl.semaphore_signal(
+            barrier, inc=1, device_id={"tile": far_first(step)}, device_id_type=MESH
+        )
+        return carry
+
+    lax.fori_loop(0, tiles - 1, greet, 0)
+    for other in (south, north):
+        pl.semaphore_signal(barrier, inc=1, device_id={"band": other}, device_id_type=MESH)
+
     loads = [
         (ocean_h, ocean.at[:, 8:24, :]), (o2w_rows_h, o2w_rows), (spectrum_h, first.at[1:9, 8:24, :]),
-        (w2o_rows_h, marks.at[my_place * groups + my_group]), (moments_h, moments), (source_h, source),
+        (w2o_rows_h, w2o_rows), (moments_h, moments), (source_h, source),
         (o2w_index_h, o2w_index), (o2w_weight_h, o2w_weight), (speed_h, speed), (wheel_h, wheel),
         (wheel_index_h, wheel_index), (wet_h, wet), (coriolis_h, coriolis), (w2o_index_h, w2o_index),
         (w2o_weight_h, w2o_weight),
@@ -69,22 +81,12 @@
     for load in loads:
         load.start()
 
-    barrier = pltpu.get_barrier_semaphore()
-
-    def greet(step, carry):
-        pl.semaphore_signal(
-            barrier, inc=1, device_id={"tile": lax.rem(tile + step, tiles)}, device_id_type=MESH
-        )
-        return carry
-
-    lax.fori_loop(1, tiles, greet, 0)
-    for other in (south, north):
-        pl.semaphore_signal(barrier, inc=1, device_id={"band": other}, device_id_type=MESH)
-
     loads[0].wait()
     loads[1].wait()
     pad_rows[...] = jnp.zeros_like(pad_rows)
     pad_rows[0:2, 0:tiles] = o2w_rows[...]
+    loads[3].wait()
+    pad_rows[2:3, 0:tiles] = w2o_rows[...]
     wanted = jnp.transpose(pad_rows[...].astype(jnp.float32))
     for slot in range(2):
         row = jnp.broadcast_to(wanted[0:tiles, slot : slot + 1], (tiles, LANES))
@@ -96,22 +98,61 @@
             north_part = jnp.where(here, ocean[levels, 8 + r : 9 + r, :], north_part)
         outgoing[:, 2 * slot, :] = east_part
         outgoing[:, 2 * slot + 1, :] = north_part
+    marks[...] = jnp.where(jnp.broadcast_to(wanted[0:tiles, 2:3], (tiles, LANES)) < 1.0, 1.0, 0.0)
+
+    for load in (4, 8, 9, 10):
+        loads[load].wait()
+    pad_small[...] = jnp.zeros_like(pad_small)
+    pad_small[0:1, 0:NFREQ] = speed[...]
+    speeds = jnp.broadcast_to(pad_small[0:1, :], (8, LANES))
+    for lo, hi in chunks(speed_x.shape[1], LANES):
+        picked = lane_pick(speeds, wheel_index[:, lo:hi])
+        speed_x[:, lo:hi] = picked * wheel[0:1, lo:hi]
+        speed_y[:, lo:hi] = picked * wheel[1:2, lo:hi]
+
+    pad_moments[...] = jnp.zeros_like(pad_moments)
+    pad_moments[0:4, 0:bins] = moments[...]
+    for lo, hi in chunks(pad_moments.shape[1], LANES):
+        top = min(hi, bins)
+        part = jnp.transpose(pad_moments[:, lo:hi])
+        high = part.astype(jnp.bfloat16)
+        low = part - high.astype(jnp.float32)
+        both = high.astype(jnp.float32) + pltpu.roll(low, 8, 1)
+        moments_t[lo:top, :] = both[0 : top - lo].astype(jnp.bfloat16)
+    loads[5].wait()
+    lane = lax.broadcasted_iota(jnp.int32, (144, LANES), 1)
+
+    def mix(step, carry):
+        rows = pl.ds(pl.multiple_of(step * 144, 144), 144)
+        mixed = jnp.dot(source[rows, :], moments_t[...], preferred_element_type=jnp.float32)
+        own = moments_t[rows, :].astype(jnp.float32)
+        full = own + DT_SOURCE * mixed
+        full = jnp.where(lane < 8, full + pltpu.roll(full, LANES - 8, 1), 0.0)
+        high = full.astype(jnp.bfloat16)
+        low = full - high.astype(jnp.float32)
+        both = high.astype(jnp.float32) + pltpu.roll(low, 8, 1)
+        mixed_t[rows, :] = both.astype(jnp.bfloat16)
+        return carry
+
+    lax.fori_loop(0, bins // 144, mix, 0)
+
     pl.semaphore_wait(barrier, tiles + 1)
 
     keep = pltpu.make_async_copy(outgoing.at[tile], incoming.at[tile], recv_sem.at[0])
     keep.start()
 
-    def give(step, carry):
-        half = (step + 1) // 2
-        reach = tiles // 2 + half * (1 - 2 * (step % 2))
-        target = lax.rem(tile + reach, tiles)
-        pltpu.make_async_remote_copy(
-            src_ref=outgoing.at[target], dst_ref=incoming.at[tile], send_sem=send_sem.at[0],
-            recv_sem=recv_sem.at[0], device_id={"tile": target}, device_id_type=MESH,
-        ).start()
-        return carry
-
-    lax.fori_loop(0, tiles - 1, give, 0)
+    def push(index, source, target):
+        def give(step, carry):
+            other = far_first(step)
+            pltpu.make_async_remote_copy(
+                src_ref=source.at[other], dst_ref=target.at[tile], send_sem=send_sem.at[index],
+                recv_sem=recv_sem.at[index], device_id={"tile": other}, device_id_type=MESH,
+            ).start()
+            return carry
+
+        lax.fori_loop(0, tiles - 1, give, 0)
+
+    push(0, outgoing, incoming)
 
     def send(index, src, dst, where):
         copy = pltpu.make_async_remote_copy(
@@ -120,22 +161,6 @@
         )
         copy.start()
         return copy
-
-    def spread_far(index, ref):
-        own = my_place * groups + my_group
-        for step in range(1, groups):
-            target = lax.rem(my_group + step, groups) * group + my_place
-            send(index, ref.at[own], ref.at[own], {"tile": target})
-
-    def spread_near(index, ref):
-        own = pl.ds(my_place * groups, groups)
-        for step in range(1, group):
-            target = my_group * group + lax.rem(my_place + step, group)
-            send(index, ref.at[own], ref.at[own], {"tile": target})
-
-    def await_blocks(sem, ref, count):
-        part = ref.at[pl.ds(0, count)]
-        pltpu.make_async_copy(part, part, sem).wait()
 
     def send_edges(base, field, edge_w, edge_e, halo_w, halo_e):
         edge_w[...] = field[1:9, 8, :]
@@ -163,8 +188,6 @@
 
     loads[2].wait()
     edges = send_edges(1, first, edge_w0, edge_e0, halo_w0, halo_e0)
-    loads[3].wait()
-    spread_far(5, marks)
 
     row_lo[...] = ocean[:, 8, :]
     row_hi[...] = ocean[:, 23, :]
@@ -180,45 +203,6 @@
         send(9, column_w, arrived_e, {"tile": west}),
         send(10, column_e, arrived_w, {"tile": east}),
     ]
-
-    for load in (4, 8, 9, 10):
-        loads[load].wait()
-    pad_small[...] = jnp.zeros_like(pad_small)
-    pad_small[0:1, 0:NFREQ] = speed[...]
-    speeds = jnp.broadcast_to(pad_small[0:1, :], (8, LANES))
-    for lo, hi in chunks(speed_x.shape[1], LANES):
-        picked = lane_pick(speeds, wheel_index[:, lo:hi])
-        speed_x[:, lo:hi] = picked * wheel[0:1, lo:hi]
-        speed_y[:, lo:hi] = picked * wheel[1:2, lo:hi]
-
-    pad_moments[...] = jnp.zeros_like(pad_moments)
-    pad_moments[0:4, 0:bins] = moments[...]
-    for lo, hi in chunks(pad_moments.shape[1], LANES):
-        top = min(hi, bins)
-        part = jnp.transpose(pad_moments[:, lo:hi])
-        high = part.astype(jnp.bfloat16)
-        low = part - high.astype(jnp.float32)
-        both = high.astype(jnp.float32) + pltpu.roll(low, 8, 1)
-        moments_t[lo:top, :] = both[0 : top - lo].astype(jnp.bfloat16)
-    loads[5].wait()
-    lane = lax.broadcasted_iota(jnp.int32, (144, LANES), 1)
-
-    def mix(step, carry):
-        rows = pl.ds(pl.multiple_of(step * 144, 144), 144)
-        mixed = jnp.dot(source[rows, :], moments_t[...], preferred_element_type=jnp.float32)
-        own = moments_t[rows, :].astype(jnp.float32)
-        full = own + DT_SOURCE * mixed
-        full = jnp.where(lane < 8, full + pltpu.roll(full, LANES - 8, 1), 0.0)
-        high = full.astype(jnp.bfloat16)
-        low = full - high.astype(jnp.float32)
-        both = high.astype(jnp.float32) + pltpu.roll(low, 8, 1)
-        mixed_t[rows, :] = both.astype(jnp.bfloat16)
-        return carry
-
-    lax.fori_loop(0, bins // 144, mix, 0)
-
-    await_blocks(recv_sem.at[5], marks, groups - 1)
-    spread_near(6, marks)
 
     for copy in ocean_edges:
         copy.wait_recv()
@@ -258,14 +242,7 @@
             else:
                 turning = -rotation * ocean[n - levels, 8:24, :]
             tendency = VISCOSITY * laplace + VERT_FRICTION * vertical + turning
-            ocean_new[n] = wet_now * (here + DT_OCEAN * tendency)
-
-    await_blocks(recv_sem.at[6], marks, (group - 1) * groups)
-    mark = jnp.where(marks[:, 0, :] < 1, 1.0, 0.0)
-    column = lax.broadcasted_iota(jnp.int32, (8, tiles), 1)
-    mine = jnp.where(column == tile, 1.0, 0.0)
-    mark_lanes[...] = jnp.zeros_like(mark_lanes)
-    mark_lanes[:, 0:tiles] = lax.dot_general(mine, mark, (((1,), (1,)), ((), ())))
+            ocean_out[n] = wet_now * (here + DT_OCEAN * tendency)
 
     loads[6].wait()
     loads[7].wait()
@@ -279,7 +256,7 @@
         weight = weight + pltpu.roll(pad_index[4 + k], 16 * k, 1)
     index = index + pltpu.roll(index, 64, 1)
     weight = (weight + pltpu.roll(weight, 64, 1)).astype(jnp.float32)
-    code, spot_index = index >> 7, index & 127
+    code, spot_index = index >> 7, index & (LANES - 1)
     is_east = spot8 < 64
 
     place_edges(edges, first, halo_w0, halo_e0)
@@ -342,71 +319,58 @@
     sums = jnp.dot(rounded[...], mixed_t[...], preferred_element_type=jnp.float32)
     sums += jnp.dot(leftover[...], moments_t[...], preferred_element_type=jnp.float32)
     sums = jnp.transpose(sums + pltpu.roll(sums, LANES - 8, 1))
-    totals[my_place * groups + my_group] = sums[0:4, :]
-    spread_far(15, totals)
-    parts = chunks(bins, 256)
-    for lo, hi in parts[:3]:
-        spectrum_new[:, :, lo:hi] = react(lo, hi)
-    await_blocks(recv_sem.at[15], totals, groups - 1)
-    spread_near(16, totals)
-    for lo, hi in parts[3:]:
-        spectrum_new[:, :, lo:hi] = react(lo, hi)
-    store_spectrum = pltpu.make_async_copy(spectrum_new, spectrum_out, load_sem.at[15])
-    store_spectrum.start()
+    for q in range(4):
+        totals[:, q, :] = marks[...] * sums[q : q + 1, :]
+    keep_totals = pltpu.make_async_copy(totals.at[tile], arrived.at[tile], recv_sem.at[5])
+    keep_totals.start()
+    push(5, totals, arrived)
+    for lo, hi in chunks(bins, 256):
+        spectrum_out[:, :, lo:hi] = react(lo, hi)
 
     loads[13].wait()
     loads[14].wait()
-    await_blocks(recv_sem.at[16], totals, (group - 1) * groups)
-    marked = mark_lanes[...]
-    for half in range(2):
-        rows = slice(8 * half, 8 * half + 8)
-        spots, codes, factors = [], [], []
-        share = jnp.zeros((8, LANES), jnp.float32)
+    halves = [slice(0, 8), slice(8, 16)]
+    turns = [rotation[rows] for rows in halves]
+    spots, codes, factors = [], [], []
+    for rows in halves:
         for k in range(4):
             entry = w2o_index[k, rows, :]
-            block = entry >> 7
-            block = (block & (group - 1)) * groups + (block >> (group.bit_length() - 1))
-            factor = w2o_weight[k, rows, :].astype(jnp.float32)
-            share = share + factor
-            spots.append(entry & 127)
-            codes.append(block)
-            factors.append(factor * lane_pick(marked, block))
-
-        def pick_total(step, carry):
-            carry = list(carry)
-            for inner in range(2):
-                block = step * 2 + inner
-                tables = [jnp.broadcast_to(totals[block, q : q + 1, :], (8, LANES)) for q in range(4)]
-                for k in range(4):
+            spots.append(entry & (LANES - 1))
+            codes.append(entry >> 7)
+            factors.append(w2o_weight[k, rows, :].astype(jnp.float32))
+    pltpu.make_async_copy(arrived, arrived, recv_sem.at[5]).wait()
+
+    def pick_total(step, carry):
+        carry = list(carry)
+        for inner in range(2):
+            block = step * 2 + inner
+            tables = [jnp.broadcast_to(arrived[block, q : q + 1, :], (8, LANES)) for q in range(4)]
+            for half in range(2):
+                easts = STRESS_COEFF * tables[0] + turns[half] * tables[3]
+                norths = STRESS_COEFF * tables[1] - turns[half] * tables[2]
+                for k in range(4 * half, 4 * half + 4):
                     here = codes[k] == block
-                    for q in range(4):
-                        carry[4 * k + q] = jnp.where(here, lane_pick(tables[q], spots[k]), carry[4 * k + q])
-            return tuple(carry)
-
-        found = lax.fori_loop(
-            0, tiles // 2, pick_total, tuple(jnp.zeros((8, LANES), jnp.float32) for _ in range(16))
-        )
-        forcing = []
-        for q in range(4):
-            total = factors[0] * found[q]
-            for k in range(1, 4):
-                total = total + factors[k] * found[4 * k + q]
-            forcing.append(total / share)
-        turn = rotation[rows]
+                    carry[k] = jnp.where(here, lane_pick(easts, spots[k]), carry[k])
+                    carry[8 + k] = jnp.where(here, lane_pick(norths, spots[k]), carry[8 + k])
+        return tuple(carry)
+
+    found = lax.fori_loop(
+        0, tiles // 2, pick_total, tuple(jnp.zeros((8, LANES), jnp.float32) for _ in range(16))
+    )
+    for half, rows in enumerate(halves):
+        share, forced = factors[4 * half], [factors[4 * half] * found[4 * half + 8 * part] for part in range(2)]
+        for k in range(4 * half + 1, 4 * half + 4):
+            share = share + factors[k]
+            forced = [forced[part] + factors[k] * found[k + 8 * part] for part in range(2)]
         scale = wet_now[rows] * DT_OCEAN
-        ocean_new[0, rows, :] += scale * (STRESS_COEFF * forcing[0] + turn * forcing[3])
-        ocean_new[levels, rows, :] += scale * (STRESS_COEFF * forcing[1] - turn * forcing[2])
-    store_ocean = pltpu.make_async_copy(ocean_new, ocean_out, load_sem.at[16])
-    store_ocean.start()
+        for part in range(2):
+            ocean_out[part * levels, rows, :] += scale * (forced[part] / share)
 
     for copy in edges + ocean_edges + edges2:
         copy.wait_send()
-    await_blocks(send_sem.at[0], outgoing, tiles - 1)
-    for index, ref in ((5, marks), (15, totals)):
-        await_blocks(send_sem.at[index], ref, groups - 1)
-        await_blocks(send_sem.at[index + 1], ref, (group - 1) * groups)
-    store_spectrum.wait()
-    store_ocean.wait()
+    for index, ref in ((0, outgoing), (5, totals)):
+        sent = ref.at[pl.ds(0, tiles - 1)]
+        pltpu.make_async_copy(sent, sent, send_sem.at[index]).wait()
 
 
 def on_device(
@@ -430,7 +394,6 @@
     layers = components * levels
     height, width, bins = spectrum.shape
     padded_bins = -(-bins // LANES) * LANES
-    group = 1 << (max(tiles.bit_length() - 1, 2) // 2)
     angle = (np.arange(NDIR) + 0.5) * (2.0 * math.pi / NDIR)
     wheel = np.zeros((8, padded_bins), np.float32)
     wheel[0, :bins] = np.repeat(np.cos(angle), NFREQ)
@@ -459,9 +422,10 @@
     scratch = [
         V((layers, 32, columns), f32), V((rows, columns), i32), V((1, rows), f32), V((10, 32, bins), f32),
         V((1, NFREQ), f32), V((bins, bins), bf16), V((4, bins), f32),
-        V((2, tiles), i32), V((4, height, width), i32), V((4, height, width), i32),
+        V((2, tiles), i32), V((1, tiles), i32), V((4, height, width), i32), V((4, height, width), i32),
         V((4, rows, columns), i32), V((4, rows, columns), i32), V((8, padded_bins), f32), V((8, padded_bins), i32),
-        V((tiles, 4, LANES), f32), V((tiles, 4, LANES), f32), V((tiles, 1, tiles), i32), V((tiles, 4, LANES), f32),
+        V((tiles, 4, LANES), f32), V((tiles, 4, LANES), f32), V((tiles, LANES), f32), V((tiles, 4, LANES), f32),
+        V((tiles, 4, LANES), f32),
     ]
     scratch += [V((height, bins), f32)] * 8
     scratch += [V((layers, columns), f32)] * 4
@@ -470,22 +434,22 @@
         V((10, 32, bins), f32), V((LANES, bins), f32), V((LANES, bins), bf16), V((LANES, bins), bf16),
         V((8, padded_bins), f32), V((8, padded_bins), f32), V((height, 16, LANES), f32), V((height, 16, LANES), f32),
         V((2, LANES, layers * rows), f32), V((8, LANES), f32), V((LANES, LANES), i32), V((8, height, LANES), i32), V((LANES, padded_bins), f32),
-        V((bins, LANES), bf16), V((bins, LANES), bf16), V((8, LANES), f32),
-        V((layers, rows, columns), f32), V((height, width, bins), f32),
-        pltpu.SemaphoreType.DMA((17,)), pltpu.SemaphoreType.DMA((17,)), pltpu.SemaphoreType.DMA((17,)),
+        V((bins, LANES), bf16), V((bins, LANES), bf16),
+        pltpu.SemaphoreType.DMA((15,)), pltpu.SemaphoreType.DMA((15,)), pltpu.SemaphoreType.DMA((15,)),
     ]
-    any_space = pl.BlockSpec(memory_space=pl.ANY)
+    far_space = pl.BlockSpec(memory_space=pltpu.HBM)
+    near_space = pl.BlockSpec(memory_space=pltpu.VMEM)
     ocean_next, spectrum_next = pl.pallas_call(
-        functools.partial(kernel, tiles, bands, group),
+        functools.partial(kernel, tiles, bands),
         out_shape=(
             jax.ShapeDtypeStruct((layers, rows, columns), f32),
             jax.ShapeDtypeStruct((height, width, bins), f32),
         ),
-        in_specs=[any_space] * len(operands),
-        out_specs=(any_space, any_space),
+        in_specs=[far_space] * len(operands),
+        out_specs=(near_space, near_space),
         scratch_shapes=scratch,
         compiler_params=pltpu.CompilerParams(
-            collective_id=0, has_side_effects=True, vmem_limit_bytes=48 << 20
+            collective_id=0, has_side_effects=True, vmem_limit_bytes=63 << 20
         ),
         name="coupled_step",
     )(*operands)

time: 109 us -> 82.3 us (0.76)
  Pallas kernels: 93.6 us -> 77.8 us
  local copies, waits for them, and re-layouts: 14.1 us -> 3.58 us
    pallas_call x1, Pallas kernels: 93.6 us -> 77.8 us  [on_device(): pl.pallas_call(functools.partial(kernel, tiles, bands), out_shape=(jax.Sh...]
    unnamed x32 -> x2, local copies, waits for them, and re-layouts: 14.1 us -> 3.58 us
where the time goes in v2:
time: 82.3 us; the launch traced here: 82.1 us
  Pallas kernels  77.8 us (95%)
  local copies, waits for them, and re-layouts  3.58 us (4%)
    pallas_call x1, Pallas kernels, on_device(): pl.pallas_call(functools.partial(kernel, tiles, bands), out_shape=(jax.Sh...  77.8 us
    unnamed x2, local copies, waits for them, and re-layouts  3.58 us

profile of v2, /device:TPU:1, one launch (start us, length us, event | category | flops | bytes accessed | tf_op | source)
XLA Modules:
  0.0 82.1 jit_solution(11774540639584261578)
XLA Ops:
  0.6 77.8 %coupled_step.1 = (f32[16,16,128]{2,1,0:T(8,128)}, f32[8,16,1296]{2,1,0:T(8,128)}) custom-call(f32[16,16,128]{2,1,0:T(8,128)} %bitcast.8, s32[16,128]{1,0:T(8,128)} %wet_h.1, f32[1,16]{1,0:T(1,128)} %bitcast.11, f32[8,16,1296]{2,1,0:T(8,128)} %spectrum_h.1, f32[1,36]{1,0:T(1,128)} %bitcast.12, bf16[1296,1296]{1,0:T(8,128)(2,1)} %source_h.1, ...), custom_call_target="tpu_custom_call" | custom-call | tf_op jit(solution)/shard_map/coupled_step/pallas_call | solution.py:442
  78.5 1.6 %copy.19 = f32[2,8,16,128]{3,2,1,0:T(8,128)} copy(f32[2,8,16,128]{3,2,1,0:T(8,128)} %bitcast.9) | data formatting | bytes 262144
  80.0 2.0 %copy.20 = f32[8,16,1296]{2,1,0:T(8,128)} copy(f32[8,16,1296]{2,1,0:T(8,128)} %get-tuple-element.9) | data formatting | bytes 1327104

commit v3 on v2

--- a/solution.py
+++ b/solution.py
@@ -53,6 +53,7 @@
     bins = first.shape[2]
     layers = ocean.shape[0]
     levels = layers // 2
+    unroll = min(8, tiles)
 
     def far_first(step):
         half = (step + 1) // 2
@@ -172,11 +173,15 @@
             send(base + 3, edge_e, halo_w, {"tile": east}),
         ]
 
-    def place_edges(copies, field, halo_w, halo_e):
-        for copy in copies:
+    def place_columns(copies, field, halo_w, halo_e):
+        for copy in copies[2:]:
             copy.wait_recv()
         field[1:9, 7, :] = halo_w[...] * jnp.where(tile == 0, 0.0, 1.0)
         field[1:9, 24, :] = halo_e[...] * jnp.where(tile == tiles - 1, 0.0, 1.0)
+
+    def place_rows(copies, field):
+        for copy in copies[:2]:
+            copy.wait_recv()
 
         @pl.when(band == 0)
         def _():
@@ -259,19 +264,20 @@
     code, spot_index = index >> 7, index & (LANES - 1)
     is_east = spot8 < 64
 
-    place_edges(edges, first, halo_w0, halo_e0)
+    place_columns(edges, first, halo_w0, halo_e0)
+    place_rows(edges, first)
     pltpu.make_async_copy(incoming, incoming, recv_sem.at[0]).wait()
 
     def pick_current(step, picked):
-        for inner in range(4):
-            block = step * 4 + inner
+        for inner in range(unroll):
+            block = step * unroll + inner
             for slot in range(2):
                 a = lane_pick(jnp.broadcast_to(incoming[block, 2 * slot : 2 * slot + 1, :], (8, LANES)), spot_index)
                 c = lane_pick(jnp.broadcast_to(incoming[block, 2 * slot + 1 : 2 * slot + 2, :], (8, LANES)), spot_index)
                 picked = jnp.where(code == block * 2 + slot, jnp.where(is_east, a, c), picked)
         return picked
 
-    picked = lax.fori_loop(0, tiles // 4, pick_current, jnp.zeros((8, LANES), jnp.float32))
+    picked = lax.fori_loop(0, tiles // unroll, pick_current, jnp.zeros((8, LANES), jnp.float32))
     weighted = picked * weight
     weighted = weighted + pltpu.roll(weighted, LANES - 16, 1)
     weighted = weighted + pltpu.roll(weighted, LANES - 32, 1)
@@ -282,8 +288,9 @@
         flow_x[y] = jnp.broadcast_to(currents[0:16, y : y + 1], (16, LANES))
         flow_y[y] = jnp.broadcast_to(currents[64:80, y : y + 1], (16, LANES))
 
-    def advect(field, last):
-        def one_row(y, carry):
+    def advect(field, last, row_of, count):
+        def one_row(step, carry):
+            y = row_of(step)
             rows = pl.ds(pl.multiple_of(y * 16, 16), 16)
             current_x, current_y = flow_x[y], flow_y[y]
             for lo, hi in chunks(bins, LANES):
@@ -304,18 +311,20 @@
                     leftover[rows, lo:hi] = (result - coarse.astype(jnp.float32)).astype(jnp.bfloat16)
             return carry
 
-        lax.fori_loop(0, 8, one_row, 0)
+        lax.fori_loop(0, count, one_row, 0)
 
     def react(lo, hi):
         product = jnp.dot(rounded[...], source[:, lo:hi], preferred_element_type=jnp.float32)
         return (moved[:, lo:hi] + DT_SOURCE * product).reshape(8, 16, hi - lo)
 
-    advect(first, False)
+    advect(first, False, lambda step: step, 8)
     for lo, hi in chunks(bins, 256):
         second[1:9, 8:24, lo:hi] = react(lo, hi)
     edges2 = send_edges(11, second, edge_w1, edge_e1, halo_w1, halo_e1)
-    place_edges(edges2, second, halo_w1, halo_e1)
-    advect(second, True)
+    place_columns(edges2, second, halo_w1, halo_e1)
+    advect(second, True, lambda step: step + 1, 6)
+    place_rows(edges2, second)
+    advect(second, True, lambda step: step * 7, 2)
     sums = jnp.dot(rounded[...], mixed_t[...], preferred_element_type=jnp.float32)
     sums += jnp.dot(leftover[...], moments_t[...], preferred_element_type=jnp.float32)
     sums = jnp.transpose(sums + pltpu.roll(sums, LANES - 8, 1))
@@ -342,8 +351,8 @@
 
     def pick_total(step, carry):
         carry = list(carry)
-        for inner in range(2):
-            block = step * 2 + inner
+        for inner in range(unroll):
+            block = step * unroll + inner
             tables = [jnp.broadcast_to(arrived[block, q : q + 1, :], (8, LANES)) for q in range(4)]
             for half in range(2):
                 easts = STRESS_COEFF * tables[0] + turns[half] * tables[3]
@@ -355,7 +364,7 @@
         return tuple(carry)
 
     found = lax.fori_loop(
-        0, tiles // 2, pick_total, tuple(jnp.zeros((8, LANES), jnp.float32) for _ in range(16))
+        0, tiles // unroll, pick_total, tuple(jnp.zeros((8, LANES), jnp.float32) for _ in range(16))
     )
     for half, rows in enumerate(halves):
         share, forced = factors[4 * half], [factors[4 * half] * found[4 * half + 8 * part] for part in range(2)]
@@ -442,14 +451,14 @@
     ocean_next, spectrum_next = pl.pallas_call(
         functools.partial(kernel, tiles, bands),
         out_shape=(
-            jax.ShapeDtypeStruct((layers, rows, columns), f32),
-            jax.ShapeDtypeStruct((height, width, bins), f32),
+            pltpu.VMEM((layers, rows, columns), f32),
+            pltpu.VMEM((height, width, bins), f32),
         ),
         in_specs=[far_space] * len(operands),
         out_specs=(near_space, near_space),
         scratch_shapes=scratch,
         compiler_params=pltpu.CompilerParams(
-            collective_id=0, has_side_effects=True, vmem_limit_bytes=63 << 20
+            collective_id=0, has_side_effects=True, vmem_limit_bytes=60 << 20
         ),
         name="coupled_step",
     )(*operands)

time: 82.3 us -> 76.6 us (0.931)
  Pallas kernels: 77.8 us -> 74.3 us
  local copies, waits for them, and re-layouts: 3.58 us -> 1.52 us
    pallas_call x1, Pallas kernels: 77.8 us -> 74.3 us  [on_device(): pl.pallas_call(functools.partial(kernel, tiles, bands), out_shape=(pltpu....]
    unnamed x2, local copies, waits for them, and re-layouts: 3.58 us -> 1.52 us
where the time goes in v3:
time: 76.6 us; the launch traced here: 76.5 us
  Pallas kernels  74.3 us (97%)
  local copies, waits for them, and re-layouts  1.52 us (2%)
    pallas_call x1, Pallas kernels, on_device(): pl.pallas_call(functools.partial(kernel, tiles, bands), out_shape=(pltpu....  74.3 us

profile of v3, /device:TPU:1, one launch (start us, length us, event | category | flops | bytes accessed | tf_op | source)
XLA Modules:
  0.0 76.5 jit_solution(10304872201136677188)
XLA Ops:
  0.6 74.3 %coupled_step.1 = (f32[16,16,128]{2,1,0:T(8,128)S(1)}, f32[8,16,1296]{2,1,0:T(8,128)S(1)}) custom-call(f32[16,16,128]{2,1,0:T(8,128)} %bitcast.9, s32[16,128]{1,0:T(8,128)} %wet_h.1, f32[1,16]{1,0:T(1,128)} %bitcast.11, f32[8,16,1296]{2,1,0:T(8,128)} %spectrum_h.1, f32[1,36]{1,0:T(1,128)} %bitcast.12, bf16[1296,1296]{1,0:T(8,128)(2,1)} %source_h.1, ...), custom_call_target="tpu_custom_call" | custom-call | tf_op jit(solution)/shard_map/coupled_step/pallas_call | solution.py:451
  75.0 0.7 copy.19
  75.6 0.9 %copy.20 = f32[8,16,1296]{2,1,0:T(8,128)} copy(f32[8,16,1296]{2,1,0:T(8,128)S(1)} %get-tuple-element.7) | data formatting | bytes 1327104

commit v4 on v3

--- a/solution.py
+++ b/solution.py
@@ -39,11 +39,11 @@
     wheel_h, wheel_index_h,
     ocean_out, spectrum_out,
     ocean, wet, coriolis, first, speed, source, moments,
-    o2w_rows, w2o_rows, o2w_index, o2w_weight, w2o_index, w2o_weight, wheel, wheel_index,
-    outgoing, incoming, marks, totals, arrived,
+    o2w_rows, o2w_index, o2w_weight, w2o_index, w2o_weight, wheel, wheel_index,
+    outgoing, incoming, marks, arrived,
     edge_w0, edge_e0, halo_w0, halo_e0, edge_w1, edge_e1, halo_w1, halo_e1,
     row_lo, row_hi, halo_lo, halo_hi, column_w, column_e, arrived_w, arrived_e,
-    second, moved, rounded, leftover, speed_x, speed_y, flow_x, flow_y,
+    second, steps, moved, rounded, leftover, speed_x, speed_y, flow_x, flow_y,
     halo_column, pad_small, pad_rows, pad_index, pad_moments, moments_t, mixed_t,
     load_sem, send_sem, recv_sem,
 ):
@@ -53,7 +53,11 @@
     bins = first.shape[2]
     layers = ocean.shape[0]
     levels = layers // 2
-    unroll = min(8, tiles)
+    unroll = min(8, tiles // 2)
+    half_tiles = tiles // 2
+    chip, core = tile // 2, tile % 2
+    own = core * half_tiles + chip
+    same_core = pl.ds(core * half_tiles, half_tiles)
 
     def far_first(step):
         half = (step + 1) // 2
@@ -73,7 +77,7 @@
 
     loads = [
         (ocean_h, ocean.at[:, 8:24, :]), (o2w_rows_h, o2w_rows), (spectrum_h, first.at[1:9, 8:24, :]),
-        (w2o_rows_h, w2o_rows), (moments_h, moments), (source_h, source),
+        (w2o_rows_h, marks.at[own]), (moments_h, moments), (source_h, source),
         (o2w_index_h, o2w_index), (o2w_weight_h, o2w_weight), (speed_h, speed), (wheel_h, wheel),
         (wheel_index_h, wheel_index), (wet_h, wet), (coriolis_h, coriolis), (w2o_index_h, w2o_index),
         (w2o_weight_h, w2o_weight),
@@ -86,8 +90,6 @@
     loads[1].wait()
     pad_rows[...] = jnp.zeros_like(pad_rows)
     pad_rows[0:2, 0:tiles] = o2w_rows[...]
-    loads[3].wait()
-    pad_rows[2:3, 0:tiles] = w2o_rows[...]
     wanted = jnp.transpose(pad_rows[...].astype(jnp.float32))
     for slot in range(2):
         row = jnp.broadcast_to(wanted[0:tiles, slot : slot + 1], (tiles, LANES))
@@ -99,7 +101,6 @@
             north_part = jnp.where(here, ocean[levels, 8 + r : 9 + r, :], north_part)
         outgoing[:, 2 * slot, :] = east_part
         outgoing[:, 2 * slot + 1, :] = north_part
-    marks[...] = jnp.where(jnp.broadcast_to(wanted[0:tiles, 2:3], (tiles, LANES)) < 1.0, 1.0, 0.0)
 
     for load in (4, 8, 9, 10):
         loads[load].wait()
@@ -142,18 +143,15 @@
     keep = pltpu.make_async_copy(outgoing.at[tile], incoming.at[tile], recv_sem.at[0])
     keep.start()
 
-    def push(index, source, target):
-        def give(step, carry):
-            other = far_first(step)
-            pltpu.make_async_remote_copy(
-                src_ref=source.at[other], dst_ref=target.at[tile], send_sem=send_sem.at[index],
-                recv_sem=recv_sem.at[index], device_id={"tile": other}, device_id_type=MESH,
-            ).start()
-            return carry
-
-        lax.fori_loop(0, tiles - 1, give, 0)
-
-    push(0, outgoing, incoming)
+    def give_rows(step, carry):
+        other = far_first(step)
+        pltpu.make_async_remote_copy(
+            src_ref=outgoing.at[other], dst_ref=incoming.at[tile], send_sem=send_sem.at[0],
+            recv_sem=recv_sem.at[0], device_id={"tile": other}, device_id_type=MESH,
+        ).start()
+        return carry
+
+    lax.fori_loop(0, tiles - 1, give_rows, 0)
 
     def send(index, src, dst, where):
         copy = pltpu.make_async_remote_copy(
@@ -163,24 +161,41 @@
         copy.start()
         return copy
 
-    def send_edges(base, field, edge_w, edge_e, halo_w, halo_e):
-        edge_w[...] = field[1:9, 8, :]
-        edge_e[...] = field[1:9, 23, :]
+    def spread(index, ref):
+        def give(step, carry):
+            other = half_tiles // 2 + (step + 1) // 2 * (1 - 2 * (step % 2))
+            other = 2 * lax.rem(chip + other, half_tiles) + core
+            pltpu.make_async_remote_copy(
+                src_ref=ref.at[own], dst_ref=ref.at[own], send_sem=send_sem.at[index],
+                recv_sem=recv_sem.at[index], device_id={"tile": other}, device_id_type=MESH,
+            ).start()
+            return carry
+
+        lax.fori_loop(0, half_tiles - 1, give, 0)
+
+    def pass_on(index, ref):
+        part = ref.at[pl.ds(0, half_tiles - 1)]
+        pltpu.make_async_copy(part, part, recv_sem.at[index]).wait()
+        return send(index + 1, ref.at[same_core], ref.at[same_core], {"tile": tile + 1 - 2 * core})
+
+    def send_edges(base, field, edge_w, edge_e, halo_w, halo_e, lanes):
+        edge_w[:, lanes] = field[1:9, 8, lanes]
+        edge_e[:, lanes] = field[1:9, 23, lanes]
         return [
-            send(base, field.at[1, 8:24, :], field.at[9, 8:24, :], {"band": south}),
-            send(base + 1, field.at[8, 8:24, :], field.at[0, 8:24, :], {"band": north}),
-            send(base + 2, edge_w, halo_e, {"tile": west}),
-            send(base + 3, edge_e, halo_w, {"tile": east}),
+            send(base, field.at[1, 8:24, lanes], field.at[9, 8:24, lanes], {"band": south}),
+            send(base + 1, field.at[8, 8:24, lanes], field.at[0, 8:24, lanes], {"band": north}),
+            send(base + 2, edge_w.at[:, lanes], halo_e.at[:, lanes], {"tile": west}),
+            send(base + 3, edge_e.at[:, lanes], halo_w.at[:, lanes], {"tile": east}),
         ]
 
     def place_columns(copies, field, halo_w, halo_e):
-        for copy in copies[2:]:
+        for copy in copies[2::4] + copies[3::4]:
             copy.wait_recv()
         field[1:9, 7, :] = halo_w[...] * jnp.where(tile == 0, 0.0, 1.0)
         field[1:9, 24, :] = halo_e[...] * jnp.where(tile == tiles - 1, 0.0, 1.0)
 
     def place_rows(copies, field):
-        for copy in copies[:2]:
+        for copy in copies[0::4] + copies[1::4]:
             copy.wait_recv()
 
         @pl.when(band == 0)
@@ -192,8 +207,10 @@
             field[9, 8:24, :] = jnp.zeros((16, bins), jnp.float32)
 
     loads[2].wait()
-    edges = send_edges(1, first, edge_w0, edge_e0, halo_w0, halo_e0)
-
+    edges = send_edges(15, first, edge_w0, edge_e0, halo_w0, halo_e0, slice(0, bins))
+
+    loads[3].wait()
+    spread(1, marks)
     row_lo[...] = ocean[:, 8, :]
     row_hi[...] = ocean[:, 23, :]
     flat = ocean[:, 8:24, :].reshape(layers * 16, LANES)
@@ -266,18 +283,32 @@
 
     place_columns(edges, first, halo_w0, halo_e0)
     place_rows(edges, first)
+
+    def differences(y, carry):
+        for lo, hi in chunks(bins, LANES):
+            center = first[y + 1, 8:24, lo:hi]
+            steps[0, y, :, lo:hi] = center - first[y + 1, 7:23, lo:hi]
+            steps[1, y, :, lo:hi] = first[y + 1, 9:25, lo:hi] - center
+            steps[2, y, :, lo:hi] = center - first[y, 8:24, lo:hi]
+            steps[3, y, :, lo:hi] = first[y + 2, 8:24, lo:hi] - center
+        return carry
+
+    lax.fori_loop(0, 8, differences, 0)
+
+    def pick_current(block, picked):
+        for slot in range(2):
+            a = lane_pick(jnp.broadcast_to(incoming[block, 2 * slot : 2 * slot + 1, :], (8, LANES)), spot_index)
+            c = lane_pick(jnp.broadcast_to(incoming[block, 2 * slot + 1 : 2 * slot + 2, :], (8, LANES)), spot_index)
+            picked = jnp.where(code == block * 2 + slot, jnp.where(is_east, a, c), picked)
+        return picked
+
+    def several_currents(step, picked):
+        for inner in range(unroll):
+            picked = pick_current(step * unroll + inner, picked)
+        return picked
+
     pltpu.make_async_copy(incoming, incoming, recv_sem.at[0]).wait()
-
-    def pick_current(step, picked):
-        for inner in range(unroll):
-            block = step * unroll + inner
-            for slot in range(2):
-                a = lane_pick(jnp.broadcast_to(incoming[block, 2 * slot : 2 * slot + 1, :], (8, LANES)), spot_index)
-                c = lane_pick(jnp.broadcast_to(incoming[block, 2 * slot + 1 : 2 * slot + 2, :], (8, LANES)), spot_index)
-                picked = jnp.where(code == block * 2 + slot, jnp.where(is_east, a, c), picked)
-        return picked
-
-    picked = lax.fori_loop(0, tiles // unroll, pick_current, jnp.zeros((8, LANES), jnp.float32))
+    picked = lax.fori_loop(0, tiles // unroll, several_currents, jnp.zeros((8, LANES), jnp.float32))
     weighted = picked * weight
     weighted = weighted + pltpu.roll(weighted, LANES - 16, 1)
     weighted = weighted + pltpu.roll(weighted, LANES - 32, 1)
@@ -288,7 +319,26 @@
         flow_x[y] = jnp.broadcast_to(currents[0:16, y : y + 1], (16, LANES))
         flow_y[y] = jnp.broadcast_to(currents[64:80, y : y + 1], (16, LANES))
 
-    def advect(field, last, row_of, count):
+    def settle(rows, lo, hi, center, change, last):
+        result = center - DT_WAVE * change
+        moved[rows, lo:hi] = result
+        coarse = result.astype(jnp.bfloat16)
+        rounded[rows, lo:hi] = coarse
+        if last:
+            leftover[rows, lo:hi] = (result - coarse.astype(jnp.float32)).astype(jnp.bfloat16)
+
+    def advect_first(y, carry):
+        rows = pl.ds(pl.multiple_of(y * 16, 16), 16)
+        current_x, current_y = flow_x[y], flow_y[y]
+        for lo, hi in chunks(bins, LANES):
+            flow = speed_x[0:1, lo:hi] + current_x[:, : hi - lo]
+            change = flow * jnp.where(flow > 0.0, steps[0, y, :, lo:hi], steps[1, y, :, lo:hi])
+            flow = speed_y[0:1, lo:hi] + current_y[:, : hi - lo]
+            change += flow * jnp.where(flow > 0.0, steps[2, y, :, lo:hi], steps[3, y, :, lo:hi])
+            settle(rows, lo, hi, first[y + 1, 8:24, lo:hi], change, False)
+        return carry
+
+    def advect(field, row_of, count):
         def one_row(step, carry):
             y = row_of(step)
             rows = pl.ds(pl.multiple_of(y * 16, 16), 16)
@@ -303,12 +353,7 @@
                 change += flow * jnp.where(
                     flow > 0.0, center - field[y, 8:24, lo:hi], field[y + 2, 8:24, lo:hi] - center
                 )
-                result = center - DT_WAVE * change
-                moved[rows, lo:hi] = result
-                coarse = result.astype(jnp.bfloat16)
-                rounded[rows, lo:hi] = coarse
-                if last:
-                    leftover[rows, lo:hi] = (result - coarse.astype(jnp.float32)).astype(jnp.bfloat16)
+                settle(rows, lo, hi, center, change, True)
             return carry
 
         lax.fori_loop(0, count, one_row, 0)
@@ -317,22 +362,20 @@
         product = jnp.dot(rounded[...], source[:, lo:hi], preferred_element_type=jnp.float32)
         return (moved[:, lo:hi] + DT_SOURCE * product).reshape(8, 16, hi - lo)
 
-    advect(first, False, lambda step: step, 8)
+    lax.fori_loop(0, 8, advect_first, 0)
     for lo, hi in chunks(bins, 256):
         second[1:9, 8:24, lo:hi] = react(lo, hi)
-    edges2 = send_edges(11, second, edge_w1, edge_e1, halo_w1, halo_e1)
+    edges2 = send_edges(11, second, edge_w1, edge_e1, halo_w1, halo_e1, slice(0, bins))
+    passed_marks = pass_on(1, marks)
     place_columns(edges2, second, halo_w1, halo_e1)
-    advect(second, True, lambda step: step + 1, 6)
+    advect(second, lambda step: step + 1, 6)
     place_rows(edges2, second)
-    advect(second, True, lambda step: step * 7, 2)
+    advect(second, lambda step: step * 7, 2)
     sums = jnp.dot(rounded[...], mixed_t[...], preferred_element_type=jnp.float32)
     sums += jnp.dot(leftover[...], moments_t[...], preferred_element_type=jnp.float32)
     sums = jnp.transpose(sums + pltpu.roll(sums, LANES - 8, 1))
-    for q in range(4):
-        totals[:, q, :] = marks[...] * sums[q : q + 1, :]
-    keep_totals = pltpu.make_async_copy(totals.at[tile], arrived.at[tile], recv_sem.at[5])
-    keep_totals.start()
-    push(5, totals, arrived)
+    arrived[own] = sums[0:4, :]
+    spread(5, arrived)
     for lo, hi in chunks(bins, 256):
         spectrum_out[:, :, lo:hi] = react(lo, hi)
 
@@ -340,36 +383,50 @@
     loads[14].wait()
     halves = [slice(0, 8), slice(8, 16)]
     turns = [rotation[rows] for rows in halves]
-    spots, codes, factors = [], [], []
+    passed_marks.wait_recv()
+    mine = jnp.where(lax.broadcasted_iota(jnp.int32, (8, tiles), 1) == tile, 1.0, 0.0)
+    mark = jnp.where(marks[:, 0, :] < 1, 1.0, 0.0)
+    pad_small[...] = jnp.zeros_like(pad_small)
+    pad_small[:, 0:tiles] = lax.dot_general(mine, mark, (((1,), (1,)), ((), ())))
+    marked = pad_small[...]
+    spots, codes, factors, shares = [], [], [], []
     for rows in halves:
         for k in range(4):
             entry = w2o_index[k, rows, :]
             spots.append(entry & (LANES - 1))
-            codes.append(entry >> 7)
-            factors.append(w2o_weight[k, rows, :].astype(jnp.float32))
-    pltpu.make_async_copy(arrived, arrived, recv_sem.at[5]).wait()
-
-    def pick_total(step, carry):
+            block = entry >> 7
+            block = (block & 1) * half_tiles + (block >> 1)
+            codes.append(block)
+            factor = w2o_weight[k, rows, :].astype(jnp.float32)
+            shares.append(factor)
+            factors.append(factor * lane_pick(marked, block))
+
+    def pick_total(block, carry):
         carry = list(carry)
+        tables = [jnp.broadcast_to(arrived[block, q : q + 1, :], (8, LANES)) for q in range(4)]
+        for half in range(2):
+            easts = STRESS_COEFF * tables[0] + turns[half] * tables[3]
+            norths = STRESS_COEFF * tables[1] - turns[half] * tables[2]
+            for k in range(4 * half, 4 * half + 4):
+                here = codes[k] == block
+                carry[k] = jnp.where(here, lane_pick(easts, spots[k]), carry[k])
+                carry[8 + k] = jnp.where(here, lane_pick(norths, spots[k]), carry[8 + k])
+        return tuple(carry)
+
+    passed = pass_on(5, arrived)
+    passed.wait_recv()
+    found = tuple(jnp.zeros((8, LANES), jnp.float32) for _ in range(16))
+
+    def several_totals(step, carry):
         for inner in range(unroll):
-            block = step * unroll + inner
-            tables = [jnp.broadcast_to(arrived[block, q : q + 1, :], (8, LANES)) for q in range(4)]
-            for half in range(2):
-                easts = STRESS_COEFF * tables[0] + turns[half] * tables[3]
-                norths = STRESS_COEFF * tables[1] - turns[half] * tables[2]
-                for k in range(4 * half, 4 * half + 4):
-                    here = codes[k] == block
-                    carry[k] = jnp.where(here, lane_pick(easts, spots[k]), carry[k])
-                    carry[8 + k] = jnp.where(here, lane_pick(norths, spots[k]), carry[8 + k])
-        return tuple(carry)
-
-    found = lax.fori_loop(
-        0, tiles // unroll, pick_total, tuple(jnp.zeros((8, LANES), jnp.float32) for _ in range(16))
-    )
+            carry = pick_total(step * unroll + inner, carry)
+        return carry
+
+    found = lax.fori_loop(0, tiles // unroll, several_totals, found)
     for half, rows in enumerate(halves):
-        share, forced = factors[4 * half], [factors[4 * half] * found[4 * half + 8 * part] for part in range(2)]
+        share, forced = shares[4 * half], [factors[4 * half] * found[4 * half + 8 * part] for part in range(2)]
         for k in range(4 * half + 1, 4 * half + 4):
-            share = share + factors[k]
+            share = share + shares[k]
             forced = [forced[part] + factors[k] * found[k + 8 * part] for part in range(2)]
         scale = wet_now[rows] * DT_OCEAN
         for part in range(2):
@@ -377,9 +434,11 @@
 
     for copy in edges + ocean_edges + edges2:
         copy.wait_send()
-    for index, ref in ((0, outgoing), (5, totals)):
-        sent = ref.at[pl.ds(0, tiles - 1)]
+    for index, ref, count in ((0, outgoing, tiles - 1), (1, marks, half_tiles - 1), (5, arrived, half_tiles - 1)):
+        sent = ref.at[pl.ds(0, count)]
         pltpu.make_async_copy(sent, sent, send_sem.at[index]).wait()
+    passed_marks.wait_send()
+    passed.wait_send()
 
 
 def on_device(
@@ -431,20 +490,19 @@
     scratch = [
         V((layers, 32, columns), f32), V((rows, columns), i32), V((1, rows), f32), V((10, 32, bins), f32),
         V((1, NFREQ), f32), V((bins, bins), bf16), V((4, bins), f32),
-        V((2, tiles), i32), V((1, tiles), i32), V((4, height, width), i32), V((4, height, width), i32),
+        V((2, tiles), i32), V((4, height, width), i32), V((4, height, width), i32),
         V((4, rows, columns), i32), V((4, rows, columns), i32), V((8, padded_bins), f32), V((8, padded_bins), i32),
-        V((tiles, 4, LANES), f32), V((tiles, 4, LANES), f32), V((tiles, LANES), f32), V((tiles, 4, LANES), f32),
-        V((tiles, 4, LANES), f32),
+        V((tiles, 4, LANES), f32), V((tiles, 4, LANES), f32), V((tiles, 1, tiles), i32), V((tiles, 4, LANES), f32),
     ]
     scratch += [V((height, bins), f32)] * 8
     scratch += [V((layers, columns), f32)] * 4
     scratch += [V((8, layers * rows), f32)] * 4
     scratch += [
-        V((10, 32, bins), f32), V((LANES, bins), f32), V((LANES, bins), bf16), V((LANES, bins), bf16),
+        V((10, 32, bins), f32), V((4, height, 16, bins), f32), V((LANES, bins), f32), V((LANES, bins), bf16), V((LANES, bins), bf16),
         V((8, padded_bins), f32), V((8, padded_bins), f32), V((height, 16, LANES), f32), V((height, 16, LANES), f32),
         V((2, LANES, layers * rows), f32), V((8, LANES), f32), V((LANES, LANES), i32), V((8, height, LANES), i32), V((LANES, padded_bins), f32),
         V((bins, LANES), bf16), V((bins, LANES), bf16),
-        pltpu.SemaphoreType.DMA((15,)), pltpu.SemaphoreType.DMA((15,)), pltpu.SemaphoreType.DMA((15,)),
+        pltpu.SemaphoreType.DMA((15,)), pltpu.SemaphoreType.DMA((23,)), pltpu.SemaphoreType.DMA((23,)),
     ]
     far_space = pl.BlockSpec(memory_space=pltpu.HBM)
     near_space = pl.BlockSpec(memory_space=pltpu.VMEM)

time: 76.6 us -> 74.3 us (0.970)
  Pallas kernels: 74.3 us -> 72 us
    pallas_call x1, Pallas kernels: 74.3 us -> 72 us  [on_device(): pl.pallas_call(functools.partial(kernel, tiles, bands), out_shape=(pltpu....]
where the time goes in v4:
time: 74.3 us; the launch traced here: 74.2 us
  Pallas kernels  72 us (97%)
  local copies, waits for them, and re-layouts  1.52 us (2%)
    pallas_call x1, Pallas kernels, on_device(): pl.pallas_call(functools.partial(kernel, tiles, bands), out_shape=(pltpu....  72 us
    unnamed x2, local copies, waits for them, and re-layouts  1.52 us

profile of v4, /device:TPU:1, one launch (start us, length us, event | category | flops | bytes accessed | tf_op | source)
XLA Modules:
  0.0 74.2 jit_solution(4366863851733735311)
XLA Ops:
  0.6 72.0 %coupled_step.1 = (f32[16,16,128]{2,1,0:T(8,128)S(1)}, f32[8,16,1296]{2,1,0:T(8,128)S(1)}) custom-call(f32[16,16,128]{2,1,0:T(8,128)} %bitcast.9, s32[16,128]{1,0:T(8,128)} %wet_h.1, f32[1,16]{1,0:T(1,128)} %bitcast.11, f32[8,16,1296]{2,1,0:T(8,128)} %spectrum_h.1, f32[1,36]{1,0:T(1,128)} %bitcast.12, bf16[1296,1296]{1,0:T(8,128)(2,1)} %source_h.1, ...), custom_call_target="tpu_custom_call" | custom-call | tf_op jit(solution)/shard_map/coupled_step/pallas_call | solution.py:509
  72.7 0.7 copy.19
  73.3 0.9 %copy.20 = f32[8,16,1296]{2,1,0:T(8,128)} copy(f32[8,16,1296]{2,1,0:T(8,128)S(1)} %get-tuple-element.7) | data formatting | bytes 1327104
